TPU v7x, 32 devices: a whole 2x2x4 slice. The times are simulated.
32 devices in a mesh: dp: 4 (over z), ctx: 4 (over y, x), tensor: 2 (over core).
Axes of the slice: x: 2, y: 2, z: 4, core: 2. Of those that a mesh axis runs over, the one named last changes fastest.
Arguments:
- tokens: bfloat16 [16, 256, 384], P('dp', 'ctx'), may hold values from -6 to 6
- cond: bfloat16 [16, 384], P('dp'), may hold values from -6 to 6
- latent_count: int32 [4], P('dp'), may hold values from 2 to 4, as said below
- cotangent: bfloat16 [16, 256, 384], P('dp', 'ctx'), may hold values from -6 to 6
- ada_w: bfloat16 [1, 384, 2304], P(None, 'dp'), may hold values from -0.3125 to 0.3125
- ada_b: bfloat16 [1, 2304], replicated, may hold values from -3 to 3
- qkv_w: bfloat16 [1, 384, 3, 6, 64], P(None, 'dp', None, 'tensor'), may hold values from -0.3125 to 0.3125
- qv_b: bfloat16 [1, 2, 6, 64], P(None, None, 'tensor'), may hold values from -1.1953125 to 1.1953125
- out_w: bfloat16 [1, 6, 64, 384], P(None, 'tensor', None, 'dp'), may hold values from -1.25 to 1.25
- out_b: bfloat16 [1, 384], replicated, may hold values from -1.1953125 to 1.1953125
- fc1_w: bfloat16 [1, 384, 1536], P(None, 'dp', 'tensor'), may hold values from -0.3125 to 0.3125
- fc1_b: bfloat16 [1, 1536], P(None, 'tensor'), may hold values from -1.796875 to 1.796875
- fc2_w: bfloat16 [1, 1536, 384], P(None, 'tensor', 'dp'), may hold values from -0.15625 to 0.15625
- fc2_b: bfloat16 [1, 384], replicated, may hold values from -1.1953125 to 1.1953125
Outputs:
- mixed: bfloat16 [16, 256, 384], P('dp', 'ctx')
- tokens_grad: float32 [16, 256, 384], P('dp', 'ctx')
- cond_grad: float32 [16, 384], P('dp')
- ada_w_grad: float32 [1, 384, 2304], P(None, 'dp')
- ada_b_grad: float32 [1, 2304], replicated
- qkv_w_grad: float32 [1, 384, 3, 6, 64], P(None, 'dp', None, 'tensor')
- qv_b_grad: float32 [1, 2, 6, 64], P(None, None, 'tensor')
- out_w_grad: float32 [1, 6, 64, 384], P(None, 'tensor', None, 'dp')
- out_b_grad: float32 [1, 384], replicated
- fc1_w_grad: float32 [1, 384, 1536], P(None, 'dp', 'tensor')
- fc1_b_grad: float32 [1, 1536], P(None, 'tensor')
- fc2_w_grad: float32 [1, 1536, 384], P(None, 'tensor', 'dp')
- fc2_b_grad: float32 [1, 384], replicated
Inputs may be any that keep to these rules, and one draw needn't show every extreme that they name: `latent_count`: the live latents of an index of dp fill its first slots of 4, the others are empty; in every draw some index holds 4.
All inputs are finite; a program needn't handle non-finite values.
Results may differ from a plain program's by a relative error of at most 0.015.
The roundings to bfloat16 on the way count: a program that leaves them out, or rounds other values in their place, can miss the bound.
Values may be sent and summed in bfloat16 or wider, within the bound.
A program may use at most 64 MiB of HBM per device.

v0:
```python
import jax
import jax.numpy as jnp
from jax import lax
from jax.sharding import PartitionSpec as P

HD = 64


EPSILON = 1e-06
PRECISE = lax.Precision.HIGHEST


def layer_norm(residual_state):
    row_mean = jnp.mean(residual_state, axis=-1, keepdims=True)
    centered = residual_state - row_mean
    inv_std = lax.rsqrt(jnp.mean(centered * centered, axis=-1, keepdims=True) + EPSILON)
    return (centered * inv_std, inv_std)


def norm_back(upstream, normed, inv_std):
    first = jnp.mean(upstream, axis=-1, keepdims=True)
    second = jnp.mean(upstream * normed, axis=-1, keepdims=True)
    return inv_std * (upstream - first - normed * second)


def split_six(modulation, model_width):
    shaped = modulation.reshape(modulation.shape[0], 6, model_width)
    return [shaped[:, slot_index][:, None, :] for slot_index in range(6)]


def tensor_total(partial_rows):
    shares = lax.psum_scatter(partial_rows, "tensor", scatter_dimension=0, tiled=True)
    return lax.all_gather(shares, "tensor", axis=0, tiled=True)


def score_block(queries, key_rows):
    score_scale = float(HD) ** (-0.5)
    return (
        jnp.einsum("lqhe,lkhe->lhqk", queries, key_rows, preferred_element_type=jnp.float32)
        * score_scale
    )


def cycle_forward(queries, key_rows, value_rows):
    latents, span_tokens, head_count, head_size = queries.shape
    initial = (
        jnp.full((latents, head_count, span_tokens), -1e30, jnp.float32),
        jnp.zeros((latents, head_count, span_tokens), jnp.float32),
        jnp.zeros((latents, head_count, span_tokens, head_size), jnp.float32),
    )

    def fold_keys(running, shard_pair, first_row):
        row_max, row_sum, accum = running
        key_part, value_part = shard_pair
        scores = score_block(queries, key_part)
        new_max = jnp.maximum(row_max, jnp.max(scores, axis=-1))
        weights = jnp.exp(scores - new_max[..., None])
        row_sum = jnp.sum(weights, axis=-1)
        update = jnp.einsum(
            "lhqk,lkhe->lhqe",
            weights.astype(jnp.bfloat16),
            value_part,
            preferred_element_type=jnp.float32,
        )
        return (new_max, row_sum, update)

    row_max, row_sum, accum = fold_keys(
        initial,
        (
            lax.all_gather(key_rows, "ctx", axis=1, tiled=True),
            lax.all_gather(value_rows, "ctx", axis=1, tiled=True),
        ),
        jnp.int32(0),
    )
    return (row_max, row_sum, accum / row_sum[..., None])


def cycle_backward(queries, key_rows, value_rows, row_max, row_sum, attn_grad, delta):
    latents, span_tokens, head_count, head_size = queries.shape
    score_scale = float(HD) ** (-0.5)
    scaled_grad = attn_grad.astype(jnp.float32) / jnp.transpose(row_sum, (0, 2, 1))[..., None]

    def block_terms(key_part, value_part):
        scores = score_block(queries, key_part)
        weights = jnp.exp(scores - row_max[..., None])
        probs = weights / row_sum[..., None]
        prob_grad = jnp.einsum(
            "lqhe,lkhe->lhqk", attn_grad, value_part, preferred_element_type=jnp.float32
        )
        score_grad = (probs * (prob_grad - delta[..., None])).astype(jnp.bfloat16)
        query_add = score_scale * jnp.einsum(
            "lhqk,lkhe->lqhe", score_grad, key_part, preferred_element_type=jnp.float32
        )
        key_grad = score_scale * jnp.einsum(
            "lhqk,lqhe->lkhe", score_grad, queries, preferred_element_type=jnp.float32
        )
        weights_low = weights.astype(jnp.bfloat16).astype(jnp.float32)
        value_grad = jnp.einsum("lhqk,lqhe->lkhe", weights_low, scaled_grad, precision=PRECISE)
        return (query_add, jnp.stack([key_grad, value_grad], axis=2))

    query_zero = jnp.zeros((latents, span_tokens, head_count, head_size), jnp.float32)
    seq_len = span_tokens * lax.axis_size("ctx")
    initial = (query_zero, jnp.zeros((latents, seq_len, 2, head_count, head_size), jnp.float32))

    def fold_keys(running, shard_pair, first_row):
        query_add, stacked_layers = block_terms(shard_pair[0], shard_pair[1])
        return (query_add, stacked_layers)

    query_grad, pair_grad = fold_keys(
        initial,
        (
            lax.all_gather(key_rows, "ctx", axis=1, tiled=True),
            lax.all_gather(value_rows, "ctx", axis=1, tiled=True),
        ),
        jnp.int32(0),
    )
    pair_local = lax.psum_scatter(pair_grad, "ctx", scatter_dimension=1, tiled=True)
    return (query_grad, pair_local)


def reduce_grads(terms):
    owned = (
        lax.psum_scatter(terms[0], "dp", scatter_dimension=0, tiled=True),
        lax.psum_scatter(terms[1], "dp", scatter_dimension=0, tiled=True),
        lax.psum_scatter(terms[2], "dp", scatter_dimension=2, tiled=True),
        lax.psum_scatter(terms[3], "dp", scatter_dimension=0, tiled=True),
        lax.psum_scatter(terms[4], "dp", scatter_dimension=1, tiled=True),
    )
    summed = lax.psum((owned[0], owned[1], owned[2], owned[3], owned[4]), "ctx")
    return summed


def per_device(
    tokens,
    cond,
    latent_count,
    cotangent,
    ada_w,
    ada_b,
    qkv_w,
    qv_b,
    out_w,
    out_b,
    fc1_w,
    fc1_b,
    fc2_w,
    fc2_b,
):
    latents, span_tokens, model_width = tokens.shape
    head_count, head_size = (qkv_w.shape[3], qkv_w.shape[4])
    inner_width = head_count * head_size
    layer_total = ada_w.shape[0]
    cond_float = cond.astype(jnp.float32)
    activated_conditioning = jax.nn.silu(cond_float).astype(jnp.bfloat16)
    live_mask = (jnp.arange(latents) < latent_count[0]).astype(jnp.float32)[:, None, None]
    row_count = latents * span_tokens
    residual_state = tokens.astype(jnp.float32)
    layer_position = 0
    gathered = (
        lax.all_gather(ada_w[layer_position], "dp", axis=0, tiled=True),
        lax.all_gather(qkv_w[layer_position], "dp", axis=0, tiled=True),
        lax.all_gather(out_w[layer_position], "dp", axis=2, tiled=True),
        lax.all_gather(fc1_w[layer_position], "dp", axis=0, tiled=True),
        lax.all_gather(fc2_w[layer_position], "dp", axis=1, tiled=True),
    )
    ada_full, qkv_full, out_full, fc1_full, fc2_full = gathered
    modulation = jnp.dot(
        activated_conditioning, ada_full, preferred_element_type=jnp.float32
    ) + ada_b[layer_position].astype(jnp.float32)
    shift_attn, scale_attn, gate_attn, shift_mlp, scale_mlp, gate_mlp = split_six(
        modulation, model_width
    )
    normed_attn, inv_attn = layer_norm(residual_state)
    attn_in = (
        (normed_attn * (1.0 + scale_attn) + shift_attn)
        .astype(jnp.bfloat16)
        .reshape(row_count, model_width)
    )
    projected = jnp.dot(
        attn_in, qkv_full.reshape(model_width, 3 * inner_width), preferred_element_type=jnp.float32
    )
    bias_pair = qv_b[layer_position].astype(jnp.float32)
    bias_rows = jnp.stack([bias_pair[0], jnp.zeros_like(bias_pair[0]), bias_pair[1]])
    qkv_rows = (
        projected.reshape(latents, span_tokens, 3, head_count, head_size) + bias_rows
    ).astype(jnp.bfloat16)
    queries = qkv_rows[:, :, 0]
    key_rows = qkv_rows[:, :, 1]
    value_rows = qkv_rows[:, :, 2]
    row_max, row_sum, attended = cycle_forward(queries, key_rows, value_rows)
    attended = jnp.transpose(attended, (0, 2, 1, 3))
    attended_low = attended.astype(jnp.bfloat16).reshape(row_count, inner_width)
    branch_part = jnp.dot(
        attended_low, out_full.reshape(inner_width, model_width), preferred_element_type=jnp.float32
    )
    branch_attn = (tensor_total(branch_part) + out_b[layer_position].astype(jnp.float32)).reshape(
        latents, span_tokens, model_width
    )
    middle = residual_state + gate_attn * branch_attn
    normed_mlp, inv_mlp = layer_norm(middle)
    mlp_in = (
        (normed_mlp * (1.0 + scale_mlp) + shift_mlp)
        .astype(jnp.bfloat16)
        .reshape(row_count, model_width)
    )
    hidden_pre = jnp.dot(mlp_in, fc1_full, preferred_element_type=jnp.float32) + fc1_b[
        layer_position
    ].astype(jnp.float32)
    hidden_act = jax.nn.gelu(hidden_pre, approximate=True).astype(jnp.bfloat16)
    mlp_part = jnp.dot(hidden_act, fc2_full, preferred_element_type=jnp.float32)
    branch_mlp = (tensor_total(mlp_part) + fc2_b[layer_position].astype(jnp.float32)).reshape(
        latents, span_tokens, model_width
    )
    saved = [
        (
            modulation,
            normed_attn,
            inv_attn,
            attn_in,
            queries,
            key_rows,
            value_rows,
            row_max,
            row_sum,
            attended,
            attended_low,
            branch_attn,
            normed_mlp,
            inv_mlp,
            mlp_in,
            hidden_pre,
            hidden_act,
            branch_mlp,
        )
    ]
    residual_state = middle + gate_mlp * branch_mlp
    mixed = (residual_state * live_mask).astype(jnp.bfloat16)
    stream_grad = cotangent.astype(jnp.float32) * live_mask
    silu_grad = jnp.zeros((latents, model_width), jnp.float32)
    weight_grads = []
    bias_grads = []
    for layer_position in reversed(range(layer_total)):
        (
            modulation,
            normed_attn,
            inv_attn,
            attn_in,
            queries,
            key_rows,
            value_rows,
            row_max,
            row_sum,
            attended,
            attended_low,
            branch_attn,
            normed_mlp,
            inv_mlp,
            mlp_in,
            hidden_pre,
            hidden_act,
            branch_mlp,
        ) = saved[layer_position]
        gathered = (
            lax.all_gather(ada_w[layer_position], "dp", axis=0, tiled=True),
            lax.all_gather(qkv_w[layer_position], "dp", axis=0, tiled=True),
            lax.all_gather(out_w[layer_position], "dp", axis=2, tiled=True),
            lax.all_gather(fc1_w[layer_position], "dp", axis=0, tiled=True),
            lax.all_gather(fc2_w[layer_position], "dp", axis=1, tiled=True),
        )
        ada_full, qkv_full, out_full, fc1_full, fc2_full = gathered
        shift_attn, scale_attn, gate_attn, shift_mlp, scale_mlp, gate_mlp = split_six(
            modulation, model_width
        )
        gate_mlp_grad = jnp.sum(stream_grad * branch_mlp, axis=1)
        mlp_grad = (stream_grad * gate_mlp).astype(jnp.bfloat16).reshape(row_count, model_width)
        fc2_b_grad = jnp.sum(mlp_grad.astype(jnp.float32), axis=0)
        fc2_w_grad = jnp.einsum(
            "rf,rd->fd", hidden_act, mlp_grad, preferred_element_type=jnp.float32
        )
        act_grad = jnp.einsum("rd,fd->rf", mlp_grad, fc2_full, preferred_element_type=jnp.float32)
        gelu_pull = jax.vjp(lambda point: jax.nn.gelu(point, approximate=True), hidden_pre)[1]
        pre_grad = gelu_pull(act_grad)[0].astype(jnp.bfloat16)
        fc1_b_grad = jnp.sum(pre_grad.astype(jnp.float32), axis=0)
        fc1_w_grad = jnp.einsum("rd,rf->df", mlp_in, pre_grad, preferred_element_type=jnp.float32)
        mlp_in_grad = tensor_total(
            jnp.einsum("rf,df->rd", pre_grad, fc1_full, preferred_element_type=jnp.float32)
        )
        mlp_in_grad = mlp_in_grad.reshape(latents, span_tokens, model_width)
        shift_mlp_grad = jnp.sum(mlp_in_grad, axis=1)
        scale_mlp_grad = jnp.sum(mlp_in_grad * normed_mlp, axis=1)
        middle_grad = stream_grad + norm_back(mlp_in_grad * (1.0 + scale_mlp), normed_mlp, inv_mlp)
        gate_attn_grad = jnp.sum(middle_grad * branch_attn, axis=1)
        branch_grad = (middle_grad * gate_attn).astype(jnp.bfloat16).reshape(row_count, model_width)
        out_b_grad = jnp.sum(branch_grad.astype(jnp.float32), axis=0)
        out_w_grad = jnp.einsum(
            "rc,rd->cd", attended_low, branch_grad, preferred_element_type=jnp.float32
        ).reshape(head_count, head_size, -1)
        attn_grad = jnp.einsum(
            "rd,cd->rc",
            branch_grad,
            out_full.reshape(inner_width, model_width),
            preferred_element_type=jnp.float32,
        )
        attn_grad = attn_grad.astype(jnp.bfloat16).reshape(
            latents, span_tokens, head_count, head_size
        )
        delta = jnp.transpose(jnp.sum(attn_grad.astype(jnp.float32) * attended, axis=-1), (0, 2, 1))
        query_grad, pair_local = cycle_backward(
            queries, key_rows, value_rows, row_max, row_sum, attn_grad, delta
        )
        qkv_grad = jnp.stack([query_grad, pair_local[:, :, 0], pair_local[:, :, 1]], axis=2).astype(
            jnp.bfloat16
        )
        flat_qkv = qkv_grad.reshape(row_count, 3 * inner_width)
        qkv_sums = jnp.sum(flat_qkv.astype(jnp.float32), axis=0).reshape(3, head_count, head_size)
        qv_b_grad = jnp.stack([qkv_sums[0], qkv_sums[2]])
        qkv_w_grad = jnp.einsum(
            "rd,rc->dc", attn_in, flat_qkv, preferred_element_type=jnp.float32
        ).reshape(-1, 3, head_count, head_size)
        attn_in_grad = tensor_total(
            jnp.einsum(
                "rc,dc->rd",
                flat_qkv,
                qkv_full.reshape(model_width, 3 * inner_width),
                preferred_element_type=jnp.float32,
            )
        )
        attn_in_grad = attn_in_grad.reshape(latents, span_tokens, model_width)
        shift_attn_grad = jnp.sum(attn_in_grad, axis=1)
        scale_attn_grad = jnp.sum(attn_in_grad * normed_attn, axis=1)
        stream_grad = middle_grad + norm_back(
            attn_in_grad * (1.0 + scale_attn), normed_attn, inv_attn
        )
        mod_grad = jnp.stack(
            [
                shift_attn_grad,
                scale_attn_grad,
                gate_attn_grad,
                shift_mlp_grad,
                scale_mlp_grad,
                gate_mlp_grad,
            ],
            axis=1,
        ).reshape(latents, 6 * model_width)
        ada_w_grad = jnp.dot(
            activated_conditioning.astype(jnp.float32).T, mod_grad, precision=PRECISE
        )
        ada_b_grad = jnp.sum(mod_grad, axis=0)
        silu_grad = jnp.dot(mod_grad, ada_full.astype(jnp.float32).T, precision=PRECISE)
        owned = reduce_grads((ada_w_grad, qkv_w_grad, out_w_grad, fc1_w_grad, fc2_w_grad))
        weight_grads.append(owned)
        bias_grads.append((ada_b_grad, qv_b_grad, out_b_grad, fc1_b_grad, fc2_b_grad))
    weight_grads = weight_grads[::-1]
    bias_grads = bias_grads[::-1]
    weight_stacks = [jnp.stack([entry[which] for entry in weight_grads]) for which in range(5)]
    bias_local = tuple((jnp.stack([entry[which] for entry in bias_grads]) for which in range(5)))
    bias_total = lax.psum(
        (bias_local[0], bias_local[1], bias_local[2], bias_local[3], bias_local[4]), ("dp", "ctx")
    )
    silu_total = lax.psum(silu_grad, "ctx")
    silu_pull = jax.vjp(jax.nn.silu, cond_float)[1]
    cond_grad = silu_pull(silu_total)[0]
    return (
        mixed,
        stream_grad,
        cond_grad,
        weight_stacks[0],
        bias_total[0],
        weight_stacks[1],
        bias_total[1],
        weight_stacks[2],
        bias_total[2],
        weight_stacks[3],
        bias_total[3],
        weight_stacks[4],
        bias_total[4],
    )


def solution(mesh):
    return jax.shard_map(
        per_device,
        mesh=mesh,
        in_specs=(
            P("dp", "ctx", None),
            P("dp", None),
            P("dp"),
            P("dp", "ctx", None),
            P(None, "dp", None),
            P(),
            P(None, "dp", None, "tensor", None),
            P(None, None, "tensor", None),
            P(None, "tensor", None, "dp"),
            P(),
            P(None, "dp", "tensor"),
            P(None, "tensor"),
            P(None, "tensor", "dp"),
            P(),
        ),
        out_specs=(
            P("dp", "ctx", None),
            P("dp", "ctx", None),
            P("dp", None),
            P(None, "dp", None),
            P(),
            P(None, "dp", None, "tensor", None),
            P(None, None, "tensor", None),
            P(None, "tensor", None, "dp"),
            P(),
            P(None, "dp", "tensor"),
            P(None, "tensor"),
            P(None, "tensor", "dp"),
            P(),
        ),
        check_vma=False,
    )
```

profile of v0, /device:TPU:0, one launch (start us, length us, event | category | flops | bytes accessed | tf_op | source)
XLA Modules:
  0.0 509.3 jit_solution(10895416982527195955)
XLA Ops:
  9.7 17.6 %all-gather.4 = bf16[1,3,64,384]{2,1,0,3:T(4,128)(2,1)S(1)} all-gather(bf16[1,3,64,96]{2,1,0,3:T(4,128)(2,1)S(1)} %copy.88), channel_id=6, replica_groups=mesh['dp'=4,'ctx'=4,'tensor'=2] {'dp'}, dimensions={3}, use_global_device_ids=true | all-gather | bytes 184320 | tf_op jit(solution)/shard_map/all_gather | solution.py:162
  27.8 42.2 %all-gather.1 = bf16[1,384,3,3,64]{4,3,2,0,1:T(4,128)(2,1)S(1)} all-gather(bf16[1,96,3,3,64]{4,3,2,0,1:T(4,128)(2,1)S(1)} %copy.81), channel_id=3, replica_groups=mesh['dp'=4,'ctx'=4,'tensor'=2] {'dp'}, dimensions={1}, use_global_device_ids=true | all-gather | bytes 552960 | tf_op jit(solution)/shard_map/all_gather | solution.py:161
  70.0 1.1 copy.82
  71.5 1.5 all-gather.9.cloned.1.call-done
  73.0 1.8 convolution_add_fusion
  75.6 11.9 %all-gather.2 = bf16[4,256,1,3,64]{4,1,3,2,0:T(8,128)(2,1)S(1)} all-gather(bf16[4,64,1,3,64]{4,1,3,2,0:T(8,128)(2,1)S(1)} %get-tuple-element.79), channel_id=4, replica_groups=mesh['dp'=4,'ctx'=4,'tensor'=2] {'ctx'}, dimensions={1}, use_global_device_ids=true | all-gather | bytes 491520 | tf_op jit(solution)/shard_map/all_gather | solution.py:70
  87.5 12.1 %all-gather.3 = bf16[4,256,1,3,64]{4,1,3,2,0:T(8,128)(2,1)S(1)} all-gather(bf16[4,64,1,3,64]{4,1,3,2,0:T(8,128)(2,1)S(1)} %get-tuple-element.80), channel_id=5, replica_groups=mesh['dp'=4,'ctx'=4,'tensor'=2] {'ctx'}, dimensions={1}, use_global_device_ids=true | all-gather | bytes 491520 | tf_op jit(solution)/shard_map/all_gather | solution.py:71
  100.6 1.3 fusion.71
  102.2 1.0 fusion.72
  103.4 16.2 %all-gather.5 = bf16[1,384,768]{2,1,0:T(8,128)(2,1)S(1)} all-gather(bf16[1,96,768]{2,1,0:T(8,128)(2,1)S(1)} %copy-done.36), channel_id=7, replica_groups=mesh['dp'=4,'ctx'=4,'tensor'=2] {'dp'}, dimensions={1}, use_global_device_ids=true | all-gather | bytes 737280 | tf_op jit(solution)/shard_map/all_gather | solution.py:163
  119.6 16.3 %all-gather.6 = bf16[1,768,384]{1,2,0:T(8,128)(2,1)} all-gather(bf16[1,768,96]{1,2,0:T(8,128)(2,1)S(1)} %copy-done.37), channel_id=8, replica_groups=mesh['dp'=4,'ctx'=4,'tensor'=2] {'dp'}, dimensions={2}, use_global_device_ids=true | all-gather | bytes 737280 | tf_op jit(solution)/shard_map/all_gather | solution.py:164
  135.9 2.3 all_gather.45
  141.2 1.2 fusion.24
  143.1 6.1 %reduce-scatter.19.cloned.1.call-done = f32[128,384]{1,0:T(8,128)} async-done(((f32[256,384]{1,0:T(8,128)}), f32[128,384]{1,0:T(8,128)}) %reduce-scatter.19.cloned.1.call-update) | async-done | bytes 196624 | tf_op jit(solution)/shard_map/reduce_scatter | solution.py:32
  149.2 2.4 all_gather.48
  151.6 1.5 convert_reduce_fusion.3
  153.2 1.3 convert_reduce_fusion.1
  154.5 1.2 fusion.28
  155.8 9.0 %reduce-scatter.21.cloned.1.call-done = f32[128,384]{1,0:T(8,128)} async-done(((f32[256,384]{1,0:T(8,128)}), f32[128,384]{1,0:T(8,128)}) %reduce-scatter.21.cloned.1.call-update) | async-done | bytes 196624 | tf_op jit(solution)/shard_map/reduce_scatter | solution.py:32
  164.8 2.3 all_gather.49
  167.9 1.6 fusion.49
  169.5 2.4 convert_reduce_fusion.4
  172.8 1.0 reshape.182
  173.8 1.3 convolution_bitcast_fusion
  176.6 1.2 fusion.5
  178.0 3.4 copy.105
  181.4 5.5 %reshape.203 = f32[256,1536]{1,0:T(8,128)} reshape(f32[256,2,4,3,64]{4,3,2,1,0:T(4,128)} %bitcast.193) | data formatting | bytes 3145728
  188.3 30.8 %reduce-scatter.31.cloned.1.call-done = f32[64,1536]{1,0:T(8,128)} async-done(((f32[256,1536]{1,0:T(8,128)}), f32[64,1536]{1,0:T(8,128)}) %reduce-scatter.31.cloned.1.call-update) | async-done | bytes 393232
  219.2 1.7 reshape.204
  222.5 1.1 fusion.73
  224.3 1.2 reshape.207
  225.9 1.4 copy.111
  227.4 1.6 fusion.65
  229.0 1.4 fusion.76
  230.5 1.1 reduce-scatter.23.cloned.1.call-done
  231.6 2.3 all_gather.50
  235.5 3.4 fusion.62
  239.0 16.7 %reduce-scatter.35.cloned.1.call-done = f32[96,192]{1,0:T(8,128)} async-done(((f32[384,192]{1,0:T(8,128)}), f32[96,192]{1,0:T(8,128)}) %reduce-scatter.35.cloned.1.call-update) | async-done | bytes 73744
  255.6 1.0 reshape.208
  257.4 25.1 %reduce-scatter.33.cloned.1.call-done = f32[96,576]{1,0:T(8,128)} async-done(((f32[384,576]{1,0:T(8,128)}), f32[96,576]{1,0:T(8,128)}) %reduce-scatter.33.cloned.1.call-update) | async-done | bytes 221200
  282.5 1.8 copy.112
  284.3 28.3 %reduce-scatter.29.cloned.1.call-done = f32[768,96]{0,1:T(8,128)} async-done(((f32[768,384]{0,1:T(8,128)}), f32[768,96]{0,1:T(8,128)}) %reduce-scatter.29.cloned.1.call-update) | async-done | bytes 294928 | tf_op jit(solution)/shard_map/reduce_scatter | solution.py:127
  312.6 30.1 %reduce-scatter.27.cloned.1.call-done = f32[96,768]{1,0:T(8,128)} async-done(((f32[384,768]{1,0:T(8,128)}), f32[96,768]{1,0:T(8,128)}) %reduce-scatter.27.cloned.1.call-update) | async-done | bytes 294928 | tf_op jit(solution)/shard_map/reduce_scatter | solution.py:126
  342.7 67.5 %reduce-scatter.25.cloned.1.call-done = f32[96,2304]{1,0:T(8,128)} async-done(((f32[384,2304]{1,0:T(8,128)}), f32[96,2304]{1,0:T(8,128)}) %reduce-scatter.25.cloned.1.call-update) | async-done | bytes 884752 | tf_op jit(solution)/shard_map/reduce_scatter | solution.py:123
  410.3 76.8 %all-reduce = (f32[1,2304]{1,0:T(1,128)}, f32[1,2,3,64]{3,2,1,0:T(4,128)S(1)}, f32[1,384]{1,0:T(1,128)}, f32[1,768]{1,0:T(1,128)}, f32[1,384]{1,0:T(1,128)}) all-reduce(f32[1,2304]{1,0:T(1,128)S(1)} %bitcast.225, f32[1,2,3,64]{3,2,1,0:T(4,128)S(1)} %maximum_bitcast_fusion, ...), channel_id=1, replica_groups=mesh['dp'=4,'ctx'=4,'tensor'=2] {'dp','ctx'}, use_global_device_ids=true, to_apply=%region_26.27 | all-reduce | flops 4224 | bytes 33792 | tf_op jit(solution)/shard_map/psum | solution.py:357
  487.7 1.5 fusion
  489.2 7.6 %psum.77 = f32[4,384]{1,0:T(4,128)S(1)} all-reduce(f32[4,384]{1,0:T(4,128)S(1)} %fusion), channel_id=1, replica_groups=mesh['dp'=4,'ctx'=4,'tensor'=2] {'ctx'}, use_global_device_ids=true, to_apply=%region_22.23 | all-reduce | flops 1536 | bytes 12288 | tf_op jit(solution)/shard_map/psum | solution.py:360
  497.4 2.2 copy.147
  (239 shorter events, 22.3 us)
Async XLA Ops:
  7.2 20.4 %copy-start.35 = (bf16[1,96,3,3,64]{1,4,3,2,0:T(8,128)(2,1)S(1)}, bf16[1,96,3,3,64]{1,4,3,2,0:T(8,128)(2,1)}, u32[]{:S(2)}) copy-start(bf16[1,96,3,3,64]{1,4,3,2,0:T(8,128)(2,1)} %param.20) | copy-start | bytes 331780
  7.2 65.8 %all-gather.9.cloned.1.call-start = ((), (), s32[]{:S(2)}) async-start(), calls=%async_computation.17 | async-start | bytes 2211840 | tf_op jit(solution)/shard_map/all_gather | solution.py:160
  7.9 127.9 %reduce-scatter.17.cloned.1.call-start = ((), (), s32[]{:S(2)}) async-start(), calls=%async_computation.10 | async-start | bytes 589824 | tf_op jit(solution)/shard_map/reduce_scatter | solution.py:32
  27.6 74.6 %copy-start.14 = (bf16[1,3,64,384]{3,2,1,0:T(8,128)(2,1)}, bf16[1,3,64,384]{3,2,1,0:T(8,128)(2,1)S(1)}, u32[]{:S(2)}) copy-start(bf16[1,3,64,384]{3,2,1,0:T(8,128)(2,1)S(1)} %copy.89) | copy-start | bytes 442372
  27.8 43.3 %copy-start.56 = (bf16[1,2304]{1,0:T(2,128)(2,1)S(1)}, bf16[1,2304]{1,0:T(2,128)(2,1)}, u32[]{:S(2)}) copy-start(bf16[1,2304]{1,0:T(2,128)(2,1)} %param.19) | copy-start | bytes 13828
  27.8 43.3 %copy-start.1 = (bf16[4,64,384]{2,1,0:T(8,128)(2,1)S(1)}, bf16[4,64,384]{2,1,0:T(8,128)(2,1)}, u32[]{:S(2)}) copy-start(bf16[4,64,384]{2,1,0:T(8,128)(2,1)} %param.14) | copy-start | bytes 589828
  27.8 45.2 %copy-start.49 = (bf16[4,384]{1,0:T(4,128)(2,1)S(1)}, bf16[4,384]{1,0:T(4,128)(2,1)}, u32[]{:S(2)}) copy-start(bf16[4,384]{1,0:T(4,128)(2,1)} %param.15) | copy-start | bytes 9220
  71.1 4.5 copy-start.4
  71.3 4.3 copy-start.42
  71.5 4.1 copy-start.47
  75.0 12.5 %copy-start.25 = (bf16[4,64,384]{2,1,0:T(8,128)(2,1)}, bf16[4,64,384]{2,1,0:T(8,128)(2,1)S(1)}, u32[]{:S(2)}) copy-start(bf16[4,64,384]{2,1,0:T(8,128)(2,1)S(1)} %fusion.39) | copy-start | bytes 589828
  75.6 24.6 %copy-start.16 = (bf16[4,64,3,3,64]{4,1,3,2,0:T(8,128)(2,1)}, bf16[4,64,3,3,64]{4,1,3,2,0:T(8,128)(2,1)S(1)}, u32[]{:S(2)}) copy-start(bf16[4,64,3,3,64]{4,1,3,2,0:T(8,128)(2,1)S(1)} %fusion.3) | copy-start | bytes 884740
  101.8 17.7 %copy-start.37 = (bf16[1,768,96]{1,2,0:T(8,128)(2,1)S(1)}, bf16[1,768,96]{1,2,0:T(8,128)(2,1)}, u32[]{:S(2)}) copy-start(bf16[1,768,96]{1,2,0:T(8,128)(2,1)} %param.26) | copy-start | bytes 442372
  103.2 46.0 %reduce-scatter.19.cloned.1.call-start = ((), (), s32[]{:S(2)}) async-start(), calls=%async_computation.11 | async-start | bytes 589824 | tf_op jit(solution)/shard_map/reduce_scatter | solution.py:32
  103.3 35.7 %copy-start.54 = (f32[384]{0:T(512)}, f32[384]{0:T(512)S(1)}, u32[]{:S(2)}) copy-start(f32[384]{0:T(512)S(1)} %convert_reduce_fusion.8) | copy-start | bytes 4612
  135.8 3.5 copy-start.39
  141.1 10.5 %copy-start.24 = (bf16[4,64,384]{2,1,0:T(8,128)(2,1)S(1)}, bf16[4,64,384]{2,1,0:T(8,128)(2,1)}, u32[]{:S(2)}) copy-start(bf16[4,64,384]{2,1,0:T(8,128)(2,1)} %param.17) | copy-start | bytes 589828
  142.4 22.4 %reduce-scatter.21.cloned.1.call-start = ((), (), s32[]{:S(2)}) async-start(), calls=%async_computation.12 | async-start | bytes 589824 | tf_op jit(solution)/shard_map/reduce_scatter | solution.py:32
  143.1 10.1 %copy-start.63 = (f32[4]{0:T(128)}, f32[4]{0:T(128)S(1)}, u32[]{:S(2)}) copy-start(f32[4]{0:T(128)S(1)} %compare_convert_fusion) | copy-start | bytes 52
  143.1 10.0 %copy-start.40 = (f32[4,1,384]{2,0,1:T(4,128)}, f32[4,1,384]{2,0,1:T(4,128)S(1)}, u32[]{:S(2)}) copy-start(f32[4,1,384]{2,0,1:T(4,128)S(1)} %copy.134) | copy-start | bytes 18436
  149.2 4.0 copy-start.20
  149.2 4.0 copy-start.28
  155.7 13.8 %copy-start.11 = (f32[256,384]{1,0:T(8,128)S(1)}, f32[256,384]{1,0:T(8,128)}, u32[]{:S(2)}) copy-start(f32[256,384]{1,0:T(8,128)} %get-tuple-element.85) | copy-start | bytes 1179652
  155.7 63.5 %reduce-scatter.31.cloned.1.call-start = ((), (), s32[]{:S(2)}) async-start(), calls=%async_computation.18 | async-start | bytes 1966080
  167.9 4.0 copy-start.15
  171.9 3.4 copy-start.6
  171.9 3.3 copy-start.29
  171.9 3.4 copy-start.23
  171.9 3.4 copy-start.46
  186.9 44.6 %reduce-scatter.23.cloned.1.call-start = ((), (), s32[]{:S(2)}) async-start(), calls=%async_computation.13 | async-start | bytes 589824 | tf_op jit(solution)/shard_map/reduce_scatter | solution.py:32
  223.7 32.0 %reduce-scatter.35.cloned.1.call-start = ((), (), s32[]{:S(2)}) async-start(), calls=%async_computation.20 | async-start | bytes 491520
  225.5 57.0 %reduce-scatter.33.cloned.1.call-start = ((), (), s32[]{:S(2)}) async-start(), calls=%async_computation.19 | async-start | bytes 1228800
  227.3 85.3 %reduce-scatter.29.cloned.1.call-start = ((), (), s32[]{:S(2)}) async-start(), calls=%async_computation.16 | async-start | bytes 1474560 | tf_op jit(solution)/shard_map/reduce_scatter | solution.py:127
  228.9 5.2 %copy-start.43 = (f32[4,64]{1,0:T(4,128)S(1)}, f32[4,64]{1,0:T(4,128)}, u32[]{:S(2)}) copy-start(f32[4,64]{1,0:T(4,128)} %copy-done.42) | copy-start | bytes 3076
  229.0 5.1 %copy-start.48 = (f32[4,64]{1,0:T(4,128)S(1)}, f32[4,64]{1,0:T(4,128)}, u32[]{:S(2)}) copy-start(f32[4,64]{1,0:T(4,128)} %copy-done.47) | copy-start | bytes 3076
  229.0 113.7 %reduce-scatter.27.cloned.1.call-start = ((), (), s32[]{:S(2)}) async-start(), calls=%async_computation.15 | async-start | bytes 1474560 | tf_op jit(solution)/shard_map/reduce_scatter | solution.py:126
  230.4 4.0 copy-start.3
  230.4 4.0 copy-start.8
  230.4 4.0 copy-start.55
  230.4 179.7 %reduce-scatter.25.cloned.1.call-start = ((), (), s32[]{:S(2)}) async-start(), calls=%async_computation.14 | async-start | bytes 4423680 | tf_op jit(solution)/shard_map/reduce_scatter | solution.py:123
  238.9 171.3 %copy-start.59 = (f32[384]{0:T(512)S(1)}, f32[384]{0:T(512)}, u32[]{:S(2)}) copy-start(f32[384]{0:T(512)} %get-tuple-element.68) | copy-start | bytes 4612
  238.9 171.3 %copy-start.61 = (f32[768]{0:T(1024)S(1)}, f32[768]{0:T(1024)}, u32[]{:S(2)}) copy-start(f32[768]{0:T(1024)} %get-tuple-element.100) | copy-start | bytes 9220
  238.9 171.3 %copy-start.60 = (f32[384]{0:T(512)S(1)}, f32[384]{0:T(512)}, u32[]{:S(2)}) copy-start(f32[384]{0:T(512)} %get-tuple-element.70) | copy-start | bytes 4612
  238.9 248.8 %copy-start = (bf16[1,384,2304]{2,1,0:T(8,128)(2,1)S(1)}, bf16[1,384,2304]{2,1,0:T(8,128)(2,1)}, u32[]{:S(2)}) copy-start(bf16[1,384,2304]{2,1,0:T(8,128)(2,1)} %all-gather.9.cloned.1.call-done) | copy-start | bytes 5308420
  238.9 258.5 %all-reduce.4.cloned.1.call-start = ((), (), s32[]{:S(2)}) async-start(), calls=%async_computation.21 | async-start | bytes 3735552 | tf_op jit(solution)/shard_map/psum | solution.py:129
  497.4 3.0 copy-start.38
  497.4 3.6 copy-start.31
  497.4 4.3 copy-start.30
  (30 other events, 49.2 us)
Sparse Core Ops, SparseCore 0:
  9.6 63.3 all-gather.8
  103.3 6.7 reduce-scatter.16
  142.5 6.6 reduce-scatter.18
  155.8 8.9 reduce-scatter.20
  187.1 32.0 reduce-scatter.30
  223.8 7.7 reduce-scatter.22
  233.9 21.7 reduce-scatter.34
  258.1 24.3 reduce-scatter.32
  284.8 27.7 reduce-scatter.28
  314.8 27.8 reduce-scatter.26
  345.0 65.0 reduce-scatter.24
  414.8 68.2 all-reduce.3
where the time goes:
time: 510 us; the launch traced here: 509 us
  waiting for transfers between devices  217 us (43%)
  blocking collectives  210 us (41%)
  local copies, waits for them, and re-layouts  32.6 us (6%)
  matrix products  22.8 us (4%)
  between operations  15.9 us (3%)
  other arithmetic  10.4 us (2%)
    psum x1, blocking collectives, per_device(): lax.psum((bias_local[0], bias_local[1], bias_local[2], bias_local[3], bia...  76.8 us
    unnamed x15, waiting for transfers between devices  73.4 us
    reduce_scatter x1, waiting for transfers between devices, reduce_grads(): lax.psum_scatter(terms[0], 'dp', scatter_dimension=0, tiled=True)  67.5 us
    all_gather x1, blocking collectives, per_device(): lax.all_gather(qkv_w[layer_position], 'dp', axis=0, tiled=True)  42.2 us
    reduce_scatter x1, waiting for transfers between devices, reduce_grads(): lax.psum_scatter(terms[3], 'dp', scatter_dimension=0, tiled=True)  30.1 us
    reduce_scatter x1, waiting for transfers between devices, reduce_grads(): lax.psum_scatter(terms[4], 'dp', scatter_dimension=1, tiled=True)  28.3 us
    unnamed x160, local copies, waits for them, and re-layouts  28 us
    all_gather x1, blocking collectives, per_device(): lax.all_gather(out_w[layer_position], 'dp', axis=2, tiled=True)  17.6 us
  transfers between devices with their start and end apart: 12, of which 10 were waited for; matrix products, arithmetic and copies ran while one was open for 4% of the time, Pallas kernels for 0%

commit v1 on v0

v1 whole, which is shorter than its diff:
```python
import jax
import jax.numpy as jnp
from jax import lax
from jax.experimental import pallas as pl
from jax.experimental.pallas import tpu as pltpu
from jax.sharding import PartitionSpec as P

HD = 64


EPSILON = 1e-06
PRECISE = lax.Precision.HIGHEST


def layer_norm(residual_state):
    row_mean = jnp.mean(residual_state, axis=-1, keepdims=True)
    centered = residual_state - row_mean
    inv_std = lax.rsqrt(jnp.mean(centered * centered, axis=-1, keepdims=True) + EPSILON)
    return (centered * inv_std, inv_std)


def norm_back(upstream, normed, inv_std):
    first = jnp.mean(upstream, axis=-1, keepdims=True)
    second = jnp.mean(upstream * normed, axis=-1, keepdims=True)
    return inv_std * (upstream - first - normed * second)


def split_six(modulation, model_width):
    shaped = modulation.reshape(modulation.shape[0], 6, model_width)
    return [shaped[:, slot_index][:, None, :] for slot_index in range(6)]


MESH = pl.DeviceIdType.MESH
ANY = pl.BlockSpec(memory_space=pl.ANY)


def peer(axis, step):
    size = lax.axis_size(axis)
    return lax.rem(lax.axis_index(axis) + step, size)


def source(axis, step):
    size = lax.axis_size(axis)
    return lax.rem(lax.axis_index(axis) + size - step, size)


def greet(axes):
    barrier = pltpu.get_barrier_semaphore()
    total = 0
    for axis in axes:
        for step in range(1, lax.axis_size(axis)):
            pl.semaphore_signal(
                barrier, inc=1, device_id={axis: peer(axis, step)}, device_id_type=MESH
            )
            total += 1
    pl.semaphore_wait(barrier, total)


def exchange(collective_id, *items):
    count = len(items)
    axes = sorted({axis for _, axis, _ in items})
    steps_of = [lax.axis_size(axis) - 1 for _, axis, _ in items]
    firsts = [sum(steps_of[:which]) for which in range(count)]
    total = sum(steps_of)

    def body(*refs):
        ins, outs = refs[:count], refs[count : 2 * count]
        send_sem, recv_sem, local_sem = refs[2 * count :]
        greet(axes)
        copies = []
        for which, (kind, axis, _) in enumerate(items):
            me = lax.axis_index(axis)
            for step in range(1, lax.axis_size(axis)):
                to = peer(axis, step)
                copy = pltpu.make_async_remote_copy(
                    src_ref=ins[which] if kind == "gather" else ins[which].at[to],
                    dst_ref=outs[which].at[me],
                    send_sem=send_sem.at[firsts[which] + step - 1],
                    recv_sem=recv_sem.at[firsts[which] + step - 1],
                    device_id={axis: to},
                    device_id_type=MESH,
                )
                copy.start()
                copies.append(copy)
        for which, (kind, axis, _) in enumerate(items):
            me = lax.axis_index(axis)
            copy = pltpu.make_async_copy(
                ins[which] if kind == "gather" else ins[which].at[me],
                outs[which].at[me],
                local_sem.at[which],
            )
            copy.start()
            copies.append(copy)
        for copy in copies:
            copy.wait()

    shapes = [
        jax.ShapeDtypeStruct(
            (lax.axis_size(axis),) + array.shape if kind == "gather" else array.shape, array.dtype
        )
        for kind, axis, array in items
    ]
    return pl.pallas_call(
        body,
        out_shape=shapes,
        in_specs=[ANY] * count,
        out_specs=[ANY] * count,
        scratch_shapes=[
            pltpu.SemaphoreType.DMA((total,)),
            pltpu.SemaphoreType.DMA((total,)),
            pltpu.SemaphoreType.DMA((count,)),
        ],
        compiler_params=pltpu.CompilerParams(collective_id=collective_id, has_side_effects=True),
        name="exchange",
    )(*[array for _, _, array in items])


def gather_weights(collective_id, shard, cond_rows):
    dp_size, ctx_size = lax.axis_size("dp"), lax.axis_size("ctx")
    far, near = dp_size - 1, ctx_size - 1

    def body(x, c, out, c_out, send_a, recv_a, send_b, recv_b, send_c, recv_c, local_sem):
        row, col = lax.axis_index("dp"), lax.axis_index("ctx")
        greet(("dp", "ctx"))
        first, conds, later = [], [], []
        for step in range(1, dp_size):
            target = {"dp": peer("dp", step)}
            copy = pltpu.make_async_remote_copy(
                c, c_out.at[row], send_c.at[step - 1], recv_c.at[step - 1], target, MESH
            )
            copy.start()
            conds.append(copy)
            copy = pltpu.make_async_remote_copy(
                x.at[col], out.at[row, col], send_a.at[step - 1], recv_a.at[step - 1], target, MESH
            )
            copy.start()
            first.append(copy)
        own = pltpu.make_async_copy(x, out.at[row], local_sem.at[0])
        own.start()
        own_cond = pltpu.make_async_copy(c, c_out.at[row], local_sem.at[1])
        own_cond.start()
        for step in range(1, dp_size):
            first[step - 1].wait_recv()
            origin = source("dp", step)
            for hop in range(1, ctx_size):
                where = (step - 1) * near + hop - 1
                copy = pltpu.make_async_remote_copy(
                    out.at[origin, col],
                    out.at[origin, col],
                    send_b.at[where],
                    recv_b.at[where],
                    {"ctx": peer("ctx", hop)},
                    MESH,
                )
                copy.start()
                later.append(copy)
        for copy in first:
            copy.wait_send()
        for copy in conds + later:
            copy.wait()
        own.wait()
        own_cond.wait()

    dma = pltpu.SemaphoreType.DMA
    return pl.pallas_call(
        body,
        out_shape=[
            jax.ShapeDtypeStruct((dp_size,) + shard.shape, shard.dtype),
            jax.ShapeDtypeStruct((dp_size,) + cond_rows.shape, cond_rows.dtype),
        ],
        in_specs=[ANY] * 2,
        out_specs=[ANY] * 2,
        scratch_shapes=[
            dma((far,)),
            dma((far,)),
            dma((far * near,)),
            dma((far * near,)),
            dma((far,)),
            dma((far,)),
            dma((2,)),
        ],
        compiler_params=pltpu.CompilerParams(collective_id=collective_id, has_side_effects=True),
        name="gather_weights",
    )(shard, cond_rows)


def tensor_total(collective_id, partial_rows):
    return jnp.sum(exchange(collective_id, ("gather", "tensor", partial_rows))[0], axis=0)


def dot_f32(left, right, left_dim, right_dim):
    return lax.dot_general(
        left, right, (((left_dim,), (right_dim,)), ((), ())), preferred_element_type=jnp.float32
    )


def per_device(
    tokens, cond, latent_count, cotangent, ada_w, ada_b, qkv_w, qv_b,
    out_w, out_b, fc1_w, fc1_b, fc2_w, fc2_b,
):
    latents, span, width = tokens.shape
    heads, head_size = qkv_w.shape[3], qkv_w.shape[4]
    inner = heads * head_size
    hidden = fc1_w.shape[2]
    shard_rows = qkv_w.shape[1]
    dp_size, ctx_size = lax.axis_size("dp"), lax.axis_size("ctx")
    rows = latents * span
    part = shard_rows // ctx_size
    f32 = lambda v: v.astype(jnp.float32)
    low = lambda v: v.astype(jnp.bfloat16)

    shard = jnp.concatenate(
        [qkv_w[0].reshape(shard_rows, 3 * inner), out_w[0].reshape(inner, shard_rows).T, fc1_w[0], fc2_w[0].T],
        axis=1,
    )
    columns = shard.shape[1]
    cond_float = f32(cond)
    silu_low = f32(low(jax.nn.silu(cond_float)))
    weights_all, silu_all = gather_weights(0, shard.reshape(ctx_size, part, columns), silu_low)
    weights_all = weights_all.reshape(width, columns)
    silu_all = silu_all.reshape(dp_size * latents, width)
    qkv_full = weights_all[:, : 3 * inner]
    out_t = weights_all[:, 3 * inner : 4 * inner]
    fc1_full = weights_all[:, 4 * inner : 4 * inner + hidden]
    fc2_t = weights_all[:, 4 * inner + hidden :]

    my_start = lax.axis_index("dp") * shard_rows
    silu_part = lax.dynamic_slice(silu_all, (0, my_start), (dp_size * latents, shard_rows))
    mod_part = dot_f32(low(silu_part), ada_w[0], 1, 0)
    (mod_parts,) = exchange(1, ("scatter", "dp", mod_part.reshape(dp_size, latents, 6 * width)))
    modulation = jnp.sum(mod_parts, axis=0) + f32(ada_b[0])
    shift_attn, scale_attn, gate_attn, shift_mlp, scale_mlp, gate_mlp = split_six(modulation, width)
    live_mask = f32(jnp.arange(latents) < latent_count[0])[:, None, None]

    stream = f32(tokens)
    normed_attn, inv_attn = layer_norm(stream)
    attn_in = low(normed_attn * (1.0 + scale_attn) + shift_attn).reshape(rows, width)
    bias_pair = f32(qv_b[0]).reshape(2, inner)
    bias_row = jnp.concatenate([bias_pair[0], jnp.zeros_like(bias_pair[0]), bias_pair[1]])
    qkv_rows = low(dot_f32(attn_in, qkv_full, 1, 0) + bias_row)
    queries = qkv_rows[:, :inner].reshape(latents, span, heads, head_size)
    (pairs,) = exchange(2, ("gather", "ctx", qkv_rows[:, inner:]))
    pairs = pairs.reshape(ctx_size, latents, span, 2, heads, head_size)
    pairs = jnp.transpose(pairs, (3, 1, 4, 0, 2, 5)).reshape(
        2, latents, heads, ctx_size * span, head_size
    )
    key_rows, value_rows = pairs[0], pairs[1]
    queries = jnp.transpose(queries, (0, 2, 1, 3))
    scale = float(HD) ** (-0.5)

    def batched(equation, left, right):
        return jnp.einsum(equation, left, right, preferred_element_type=jnp.float32)

    scores = batched("lhqe,lhke->lhqk", queries, key_rows) * scale
    weights = jnp.exp(scores - jnp.max(scores, axis=-1, keepdims=True))
    row_sum = jnp.sum(weights, axis=-1, keepdims=True)
    weights_low = low(weights)
    attended = batched("lhqk,lhke->lhqe", weights_low, value_rows) / row_sum
    attended_low = jnp.transpose(low(attended), (0, 2, 1, 3)).reshape(rows, inner)
    branch_attn = (
        tensor_total(3, dot_f32(attended_low, out_t, 1, 1)) + f32(out_b[0])
    ).reshape(latents, span, width)
    middle = stream + gate_attn * branch_attn
    normed_mlp, inv_mlp = layer_norm(middle)
    mlp_in = low(normed_mlp * (1.0 + scale_mlp) + shift_mlp).reshape(rows, width)
    hidden_pre = dot_f32(mlp_in, fc1_full, 1, 0) + f32(fc1_b[0])
    gelu_out, gelu_pull = jax.vjp(lambda point: jax.nn.gelu(point, approximate=True), hidden_pre)
    hidden_act = low(gelu_out)
    stream_grad = f32(cotangent) * live_mask
    mlp_grad = low(stream_grad * gate_mlp).reshape(rows, width)
    pre_grad = low(gelu_pull(dot_f32(mlp_grad, fc2_t, 1, 0))[0])
    both = exchange(
        4,
        ("gather", "tensor", dot_f32(hidden_act, fc2_t, 1, 1)),
        ("gather", "tensor", dot_f32(pre_grad, fc1_full, 1, 1)),
    )
    branch_mlp = (jnp.sum(both[0], axis=0) + f32(fc2_b[0])).reshape(latents, span, width)
    mlp_in_grad = jnp.sum(both[1], axis=0).reshape(latents, span, width)
    mixed = low((middle + gate_mlp * branch_mlp) * live_mask)
    gate_mlp_grad = jnp.sum(stream_grad * branch_mlp, axis=1)
    fc2_b_grad = jnp.sum(f32(mlp_grad), axis=0)
    fc2_grad_t = dot_f32(mlp_grad, hidden_act, 0, 0)
    fc1_b_grad = jnp.sum(f32(pre_grad), axis=0)
    fc1_grad = dot_f32(mlp_in, pre_grad, 0, 0)
    shift_mlp_grad = jnp.sum(mlp_in_grad, axis=1)
    scale_mlp_grad = jnp.sum(mlp_in_grad * normed_mlp, axis=1)
    middle_grad = stream_grad + norm_back(mlp_in_grad * (1.0 + scale_mlp), normed_mlp, inv_mlp)
    gate_attn_grad = jnp.sum(middle_grad * branch_attn, axis=1)
    branch_grad = low(middle_grad * gate_attn).reshape(rows, width)
    out_b_grad = jnp.sum(f32(branch_grad), axis=0)
    out_grad_t = dot_f32(branch_grad, attended_low, 0, 0)
    attn_grad = low(dot_f32(branch_grad, out_t, 1, 0)).reshape(latents, span, heads, head_size)
    attn_grad = jnp.transpose(attn_grad, (0, 2, 1, 3))
    delta = jnp.sum(f32(attn_grad) * attended, axis=-1, keepdims=True)
    prob_grad = batched("lhqe,lhke->lhqk", attn_grad, value_rows)
    score_grad = low(weights / row_sum * (prob_grad - delta))
    query_grad = low(scale * batched("lhqk,lhke->lhqe", score_grad, key_rows))
    key_grad = scale * batched("lhqk,lhqe->lhke", score_grad, queries)
    value_grad = batched("lhqk,lhqe->lhke", weights_low, low(f32(attn_grad) / row_sum))
    pair_grad = low(jnp.stack([key_grad, value_grad])).reshape(
        2, latents, heads, ctx_size, span, head_size
    )
    pair_grad = jnp.transpose(pair_grad, (3, 1, 4, 0, 2, 5)).reshape(ctx_size, rows, 2 * inner)
    (pair_parts,) = exchange(5, ("scatter", "ctx", pair_grad))
    pair_own = low(jnp.sum(f32(pair_parts), axis=0))
    flat_qkv = jnp.concatenate(
        [jnp.transpose(query_grad, (0, 2, 1, 3)).reshape(rows, inner), pair_own], axis=1
    )
    qkv_sums = jnp.sum(f32(flat_qkv), axis=0)
    qkv_grad = dot_f32(attn_in, flat_qkv, 0, 0)
    attn_in_grad = tensor_total(6, dot_f32(flat_qkv, qkv_full, 1, 1)).reshape(latents, span, width)
    shift_attn_grad = jnp.sum(attn_in_grad, axis=1)
    scale_attn_grad = jnp.sum(attn_in_grad * normed_attn, axis=1)
    tokens_grad = middle_grad + norm_back(attn_in_grad * (1.0 + scale_attn), normed_attn, inv_attn)
    mod_grad = jnp.concatenate(
        [shift_attn_grad, scale_attn_grad, gate_attn_grad, shift_mlp_grad, scale_mlp_grad, gate_mlp_grad],
        axis=1,
    )
    biases = jnp.concatenate(
        [qkv_sums[:inner], qkv_sums[2 * inner :], out_b_grad, fc1_b_grad, fc2_b_grad]
    )[None]

    all_grads = low(jnp.concatenate([qkv_grad, out_grad_t, fc1_grad, fc2_grad_t], axis=1))
    all_grads = jnp.transpose(all_grads.reshape(dp_size, ctx_size, part, columns), (1, 0, 2, 3))
    grad_parts, mod_parts, bias_parts = exchange(
        7, ("scatter", "ctx", all_grads), ("gather", "ctx", mod_grad), ("gather", "ctx", biases)
    )
    grad_part = low(jnp.sum(f32(grad_parts), axis=0))
    grad_parts, mod_all, bias_parts = exchange(
        8,
        ("scatter", "dp", grad_part),
        ("gather", "dp", jnp.sum(mod_parts, axis=0)),
        ("gather", "dp", jnp.sum(bias_parts, axis=0)),
    )
    grad_own = low(jnp.sum(f32(grad_parts), axis=0))
    bias_total = jnp.sum(bias_parts, axis=0)[0]
    mod_all = mod_all.reshape(dp_size * latents, 6 * width)
    ada_b_grad = jnp.sum(mod_all, axis=0)
    ada_w_grad = jnp.dot(silu_part.T, mod_all, precision=PRECISE)
    silu_grad = jnp.dot(mod_all, f32(ada_w[0]).T, precision=PRECISE)
    grads, silu_parts = exchange(
        9,
        ("gather", "ctx", grad_own),
        ("scatter", "dp", silu_grad.reshape(dp_size, latents, shard_rows)),
    )
    grads = f32(grads.reshape(shard_rows, columns))
    silu_total = jnp.transpose(silu_parts, (1, 0, 2)).reshape(latents, width)
    cond_grad = jax.vjp(jax.nn.silu, cond_float)[1](silu_total)[0]
    ends = [2 * inner, 2 * inner + width, 2 * inner + width + hidden]
    return (
        mixed,
        tokens_grad,
        cond_grad,
        ada_w_grad[None],
        ada_b_grad[None],
        grads[:, : 3 * inner].reshape(1, shard_rows, 3, heads, head_size),
        bias_total[: ends[0]].reshape(1, 2, heads, head_size),
        grads[:, 3 * inner : 4 * inner].T.reshape(1, heads, head_size, shard_rows),
        bias_total[ends[0] : ends[1]][None],
        grads[:, 4 * inner : 4 * inner + hidden][None],
        bias_total[ends[1] : ends[2]][None],
        grads[:, 4 * inner + hidden :].T[None],
        bias_total[ends[2] :][None],
    )


def solution(mesh):
    return jax.shard_map(
        per_device,
        mesh=mesh,
        in_specs=(
            P("dp", "ctx", None),
            P("dp", None),
            P("dp"),
            P("dp", "ctx", None),
            P(None, "dp", None),
            P(),
            P(None, "dp", None, "tensor", None),
            P(None, None, "tensor", None),
            P(None, "tensor", None, "dp"),
            P(),
            P(None, "dp", "tensor"),
            P(None, "tensor"),
            P(None, "tensor", "dp"),
            P(),
        ),
        out_specs=(
            P("dp", "ctx", None),
            P("dp", "ctx", None),
            P("dp", None),
            P(None, "dp", None),
            P(),
            P(None, "dp", None, "tensor", None),
            P(None, None, "tensor", None),
            P(None, "tensor", None, "dp"),
            P(),
            P(None, "dp", "tensor"),
            P(None, "tensor"),
            P(None, "tensor", "dp"),
            P(),
        ),
        check_vma=False,
    )
```

time: 510 us -> 254 us (0.50)
  waiting for transfers between devices: 217 us -> 0 us
  blocking collectives: 210 us -> 0 us
  Pallas kernels: 0 us -> 159 us
  other arithmetic: 10.4 us -> 34.5 us
  between operations: 15.9 us -> 2.14 us
    pallas_call x0 -> x10, Pallas kernels: none -> 159 us  [the longest x9 132 us: exchange(): pl.pallas_call(body, out_shape=shapes, in_specs=[ANY] * count, out_specs=...]
    reduce_scatter x7 -> x0, waiting for transfers between devices: 142 us -> none  [the longest x1 67.5 us: reduce_grads(): lax.psum_scatter(terms[0], 'dp', scatter_dimension=0, tiled=True)]
    all_gather x10 -> x0, blocking collectives: 126 us -> none  [the longest x1 42.2 us: per_device(): lax.all_gather(qkv_w[layer_position], 'dp', axis=0, tiled=True)]
    psum x2 -> x0, blocking collectives: 84.4 us -> none  [the longest x1 76.8 us: per_device(): lax.psum((bias_local[0], bias_local[1], bias_local[2], bias_local[3], bia...]
    unnamed x15 -> x0, waiting for transfers between devices: 73.4 us -> none
    unnamed x160 -> x61, local copies, waits for them, and re-layouts: 28 us -> 4.11 us
    reduce_sum x8 -> x17, other arithmetic: 6.54 us -> 20 us  [the longest x1 2.83 us: per_device(): out_b_grad = jnp.sum(f32(branch_grad), axis=0)]
  transfers between devices with their start and end apart: 12 -> 0, of which waited for: 10 -> 0; matrix products, arithmetic and copies ran while one was open for 4% -> 0% of each run, Pallas kernels for 0% -> 0%
where the time goes in v1:
time: 254 us; the launch traced here: 252 us
  Pallas kernels  159 us (63%)
  other arithmetic  34.5 us (14%)
  local copies, waits for them, and re-layouts  29.6 us (12%)
  matrix products  27.3 us (11%)
    pallas_call x9, Pallas kernels, exchange(): pl.pallas_call(body, out_shape=shapes, in_specs=[ANY] * count, out_specs=...  132 us
    pallas_call x1, Pallas kernels, gather_weights(): pl.pallas_call(body, out_shape=[jax.ShapeDtypeStruct((dp_size,) + shard.s...  26.6 us
    dot_general x13, matrix products, dot_f32(): lax.dot_general(left, right, (((left_dim,), (right_dim,)), ((), ())), pre...  18.8 us

profile of v1, /device:TPU:0, one launch (start us, length us, event | category | flops | bytes accessed | tf_op | source)
XLA Modules:
  0.0 252.2 jit_solution(176248591670176278)
XLA Ops:
  1.4 1.3 convert_reduce_fusion.8
  2.7 1.3 convert_reduce_fusion.7
  3.9 1.0 convert_reduce_fusion.1
  5.0 1.1 fusion.44
  7.1 1.3 convert_reduce_fusion.6
  8.4 1.3 fusion.81.c
  11.3 1.1 copy.73
  12.7 1.9 concatenate.35.x
  14.5 26.6 %gather_weights.1 = (bf16[4,4,24,2304]{3,2,1,0:T(8,128)(2,1)}, f32[4,4,384]{2,1,0:T(4,128)}) custom-call(bf16[4,24,2304]{2,1,0:T(8,128)(2,1)} %concatenate.35.x, f32[4,384]{1,0:T(4,128)} %fusion.81.c), custom_call_target="tpu_custom_call" | custom-call | tf_op jit(solution)/shard_map/gather_weights/pallas_call | solution.py:165
  42.8 6.9 %exchange.9 = f32[4,4,2304]{2,1,0:T(4,128)} custom-call(f32[4,4,2304]{2,1,0:T(4,128)} %fusion.32.refs_0_), custom_call_target="tpu_custom_call" | custom-call | tf_op jit(solution)/shard_map/exchange/pallas_call | solution.py:103
  53.3 1.4 fusion.3
  55.6 10.8 %exchange.10 = bf16[4,256,384]{2,1,0:T(8,128)(2,1)} custom-call(bf16[256,384]{1,0:T(8,128)(2,1)} %slice.121.refs_0_), custom_call_target="tpu_custom_call" | custom-call | tf_op jit(solution)/shard_map/exchange/pallas_call | solution.py:103
  66.4 1.4 copy.78
  72.1 1.1 fusion.49
  74.4 2.1 fusion.63.refs_0_
  76.4 13.0 %exchange.11 = f32[2,256,384]{2,1,0:T(8,128)} custom-call(f32[256,384]{1,0:T(8,128)} %fusion.63.refs_0_), custom_call_target="tpu_custom_call" | custom-call | tf_op jit(solution)/shard_map/exchange/pallas_call | solution.py:103
  89.5 1.2 reduce_sum.312
  91.4 1.4 convolution_add_fusion
  92.8 2.6 %convert_reduce_fusion = (f32[768]{0:T(1024)}, bf16[256,768]{1,0:T(8,128)(2,1)S(1)}) fusion(f32[256,768]{1,0:T(8,128)S(1)} %convolution_add_fusion, bf16[256,384]{1,0:T(8,128)(2,1)} %bitcast.179, bf16[384,2304]{1,0:T(8,128)(2,1)} %bitcast.172), kind=kOutput, calls=%fused_computation.29 | convolution fusion | flops 155319552 | bytes 1969152 | tf_op jit(solution)/shard_map/dot_general | solution.py:192
  95.4 1.1 convolution_convert_fusion.1
  96.6 1.1 fusion.21.refs_1_
  97.7 1.3 convolution_convert_fusion
  99.0 1.1 fusion.17.refs_0_
  100.2 25.5 %exchange.12 = (f32[2,256,384]{2,1,0:T(8,128)}, f32[2,256,384]{2,1,0:T(8,128)}) custom-call(f32[256,384]{1,0:T(8,128)} %fusion.17.refs_0_, f32[256,384]{1,0:T(8,128)} %fusion.21.refs_1_), custom_call_target="tpu_custom_call" | custom-call | tf_op jit(solution)/shard_map/exchange/pallas_call | solution.py:103
  125.7 2.0 reduce_sum.316
  127.6 1.2 reduce_sum.318
  129.6 2.8 %convert_reduce_fusion.4 = (f32[384]{0:T(512)}, bf16[4,64,384]{2,1,0:T(8,128)(2,1)S(1)}, f32[4,64,384]{2,1,0:T(8,128)}, bf16[4,64,384]{2,1,0:T(8,128)(2,1)}, f32[4,384]{1,0:T(4,128)}) fusion(f32[4,384]{1,0:T(4,128)S(1)} %get-tuple-element.95, f32[4,64]{1,0:T(4,128)S(1)} %broadcast_multiply_fusion.2, f32[4,64,384]{2,1,0:T(8,128)S(1)} %get-tuple-element.81, ...), kind=kLoop, calls=%fused_computation.80 | loop fusion | flops 2062464 | bytes 2194448 | tf_op jit(solution)/shard_map/reduce_sum | solution.py:290
  132.5 1.3 convolution_convert_fusion.5
  133.9 1.1 fusion.45
  135.0 1.5 fusion.1
  136.5 1.1 convolution_convert_fusion.3
  141.5 1.5 maximum_bitcast_fusion
  144.1 1.2 copy.88.refs_0_
  145.2 12.3 %exchange.13 = bf16[4,256,384]{2,1,0:T(8,128)(2,1)} custom-call(bf16[4,256,384]{2,1,0:T(8,128)(2,1)} %copy.88.refs_0_), custom_call_target="tpu_custom_call" | custom-call | tf_op jit(solution)/shard_map/exchange/pallas_call | solution.py:103
  157.6 1.3 reduce_sum.322
  159.0 2.3 fusion.34.refs_0_
  162.2 1.3 convolution_convert_fusion.2
  163.5 2.0 concatenate.38
  165.5 13.1 %exchange.14 = f32[2,256,384]{2,1,0:T(8,128)} custom-call(f32[256,384]{1,0:T(8,128)} %fusion.34.refs_0_), custom_call_target="tpu_custom_call" | custom-call | tf_op jit(solution)/shard_map/exchange/pallas_call | solution.py:103
  178.6 1.2 reduce_sum.323
  181.8 25.4 %exchange.15 = (bf16[4,4,24,2304]{3,2,1,0:T(8,128)(2,1)}, f32[4,4,2304]{2,1,0:T(4,128)}, f32[4,1,1920]{2,1,0:T(1,128)}) custom-call(bf16[4,4,24,2304]{3,2,1,0:T(8,128)(2,1)} %bitcast.160, f32[4,2304]{1,0:T(4,128)} %copy-done.14, f32[1,1920]{1,0:T(1,128)} %broadcast_in_dim.13.refs_2_), custom_call_target="tpu_custom_call" | custom-call | tf_op jit(solution)/shard_map/exchange/pallas_call | solution.py:103
  207.2 2.7 %reduce_sum.336.refs_0_ = bf16[4,24,2304]{2,1,0:T(8,128)(2,1)} reduce(bf16[4,4,24,2304]{3,2,1,0:T(8,128)(2,1)} %get-tuple-element.29, bf16[]{:T(256)} %constant.52.clone.1), dimensions={0}, to_apply=%region_27.28 | reduce | flops 663552 | bytes 2211842 | tf_op jit(solution)/shard_map/reduce_sum | solution.py:328
  211.2 17.3 %exchange.16 = (bf16[4,24,2304]{2,1,0:T(8,128)(2,1)}, f32[4,4,2304]{2,1,0:T(4,128)}, f32[4,1,1920]{2,1,0:T(1,128)}) custom-call(bf16[4,24,2304]{2,1,0:T(8,128)(2,1)} %reduce_sum.336.refs_0_, f32[4,2304]{1,0:T(4,128)} %reduce_sum.337.refs_1_, f32[1,1920]{1,0:T(1,128)} %reduce_sum.339.refs_2_), custom_call_target="tpu_custom_call" | custom-call | tf_op jit(solution)/shard_map/exchange/pallas_call | solution.py:103
  228.5 1.8 reduce_sum.340.refs_0_
  232.8 2.0 fusion.30.refs_1_
  237.4 7.9 %exchange.17 = (bf16[4,24,2304]{2,1,0:T(8,128)(2,1)}, f32[4,4,96]{2,1,0:T(4,128)}) custom-call(bf16[24,2304]{1,0:T(8,128)(2,1)} %reduce_sum.340.refs_0_, f32[4,4,96]{2,1,0:T(4,128)} %fusion.30.refs_1_), custom_call_target="tpu_custom_call" | custom-call | tf_op jit(solution)/shard_map/exchange/pallas_call | solution.py:103
  246.7 1.9 convolution_bitcast_fusion
  248.6 1.1 bitcast_convert_fusion
  (144 shorter events, 34.0 us)
Async XLA Ops:
  0.6 41.3 %copy-start = (bf16[1,96,2304]{2,1,0:T(8,128)(2,1)S(1)}, bf16[1,96,2304]{2,1,0:T(8,128)(2,1)}, u32[]{:S(2)}) copy-start(bf16[1,96,2304]{2,1,0:T(8,128)(2,1)} %param.18) | copy-start | bytes 1327108
  1.4 49.4 %copy-start.25 = (f32[4]{0:T(128)}, f32[4]{0:T(128)S(1)}, u32[]{:S(2)}) copy-start(f32[4]{0:T(128)S(1)} %compare_convert_fusion) | copy-start | bytes 52
  11.3 39.5 %copy-start.1 = (bf16[4,64,384]{2,1,0:T(8,128)(2,1)S(1)}, bf16[4,64,384]{2,1,0:T(8,128)(2,1)}, u32[]{:S(2)}) copy-start(bf16[4,64,384]{2,1,0:T(8,128)(2,1)} %param.14) | copy-start | bytes 589828
  11.3 39.5 %copy-start.6 = (bf16[4,64,384]{2,1,0:T(8,128)(2,1)S(1)}, bf16[4,64,384]{2,1,0:T(8,128)(2,1)}, u32[]{:S(2)}) copy-start(bf16[4,64,384]{2,1,0:T(8,128)(2,1)} %param.17) | copy-start | bytes 589828
  51.6 14.8 %copy-start.7 = (bf16[4,64,384]{2,1,0:T(8,128)(2,1)}, bf16[4,64,384]{2,1,0:T(8,128)(2,1)S(1)}, u32[]{:S(2)}) copy-start(bf16[4,64,384]{2,1,0:T(8,128)(2,1)S(1)} %get-tuple-element.76) | copy-start | bytes 589828
  71.4 1.8 copy-start.9
  73.3 17.4 %copy-start.18 = (f32[384]{0:T(512)S(1)}, f32[384]{0:T(512)}, u32[]{:S(2)}) copy-start(f32[384]{0:T(512)} %convert_reduce_fusion.8) | copy-start | bytes 4612
  89.5 1.9 copy-start.20
  92.8 3.7 %copy-start.4 = (bf16[4,4,24,2304]{3,2,1,0:T(8,128)(2,1)S(1)}, bf16[4,4,24,2304]{3,2,1,0:T(8,128)(2,1)}, u32[]{:S(2)}) copy-start(bf16[4,4,24,2304]{3,2,1,0:T(8,128)(2,1)} %get-tuple-element.26) | copy-start | bytes 5308420
  95.4 2.3 copy-start.12
  137.6 1.1 copy-start.11
  138.6 2.0 copy-start.10
  157.5 3.9 %copy-start.22 = (f32[384]{0:T(512)S(1)}, f32[384]{0:T(512)}, u32[]{:S(2)}) copy-start(f32[384]{0:T(512)} %get-tuple-element.75) | copy-start | bytes 4612
  157.5 3.9 %copy-start.23 = (f32[384]{0:T(512)S(1)}, f32[384]{0:T(512)}, u32[]{:S(2)}) copy-start(f32[384]{0:T(512)} %get-tuple-element.77) | copy-start | bytes 4612
  157.5 3.9 %copy-start.24 = (f32[768]{0:T(1024)S(1)}, f32[768]{0:T(1024)}, u32[]{:S(2)}) copy-start(f32[768]{0:T(1024)} %get-tuple-element.105) | copy-start | bytes 9220
  158.8 4.6 %copy-start.2 = (bf16[4,4,24,768]{3,2,0,1:T(8,128)(2,1)S(1)}, bf16[4,4,24,768]{3,2,0,1:T(8,128)(2,1)}, u32[]{:S(2)}) copy-start(bf16[4,4,24,768]{3,2,0,1:T(8,128)(2,1)} %convolution_convert_fusion.1) | copy-start | bytes 1769476
  158.9 4.6 %copy-start.5 = (bf16[4,4,24,192]{3,2,0,1:T(8,128)(2,1)S(1)}, bf16[4,4,24,192]{3,2,0,1:T(8,128)(2,1)}, u32[]{:S(2)}) copy-start(bf16[4,4,24,192]{3,2,0,1:T(8,128)(2,1)} %convolution_convert_fusion.4) | copy-start | bytes 442372
  158.9 4.6 %copy-start.8 = (bf16[4,4,24,768]{3,2,0,1:T(8,128)(2,1)S(1)}, bf16[4,4,24,768]{3,2,0,1:T(8,128)(2,1)}, u32[]{:S(2)}) copy-start(bf16[4,4,24,768]{3,2,0,1:T(8,128)(2,1)} %convolution_convert_fusion) | copy-start | bytes 1769476
  165.5 14.6 %copy-start.3 = (f32[4,64,384]{2,1,0:T(8,128)S(1)}, f32[4,64,384]{2,1,0:T(8,128)}, u32[]{:S(2)}) copy-start(f32[4,64,384]{2,1,0:T(8,128)} %get-tuple-element.79) | copy-start | bytes 1179652
  165.5 14.6 %copy-start.19 = (f32[384]{0:T(512)S(1)}, f32[384]{0:T(512)}, u32[]{:S(2)}) copy-start(f32[384]{0:T(512)} %convert_reduce_fusion.8) | copy-start | bytes 4612
  178.6 2.6 %copy-start.16 = (f32[4,384]{1,0:T(4,128)S(1)}, f32[4,384]{1,0:T(4,128)}, u32[]{:S(2)}) copy-start(f32[4,384]{1,0:T(4,128)} %get-tuple-element.68) | copy-start | bytes 18436
  178.6 2.6 %copy-start.17 = (f32[4,384]{1,0:T(4,128)S(1)}, f32[4,384]{1,0:T(4,128)}, u32[]{:S(2)}) copy-start(f32[4,384]{1,0:T(4,128)} %get-tuple-element.89) | copy-start | bytes 18436
  181.2 0.6 copy-start.14
  207.2 2.7 %copy-start.15 = (f32[4,1,1920]{2,1,0:T(1,128)S(1)}, f32[4,1,1920]{2,1,0:T(1,128)}, u32[]{:S(2)}) copy-start(f32[4,1,1920]{2,1,0:T(1,128)} %get-tuple-element.31) | copy-start | bytes 92164
  207.2 3.3 %copy-start.13 = (f32[4,4,2304]{2,1,0:T(4,128)S(1)}, f32[4,4,2304]{2,1,0:T(4,128)}, u32[]{:S(2)}) copy-start(f32[4,4,2304]{2,1,0:T(4,128)} %get-tuple-element.30) | copy-start | bytes 442372
  209.9 36.2 %copy-start.21 = (bf16[4,384]{1,0:T(4,128)(2,1)S(1)}, bf16[4,384]{1,0:T(4,128)(2,1)}, u32[]{:S(2)}) copy-start(bf16[4,384]{1,0:T(4,128)(2,1)} %param.15) | copy-start | bytes 9220

commit v2 on v1

--- a/solution.py
+++ b/solution.py
@@ -31,7 +31,7 @@
 
 
 MESH = pl.DeviceIdType.MESH
-ANY = pl.BlockSpec(memory_space=pl.ANY)
+VMEM = pl.BlockSpec(memory_space=pltpu.VMEM)
 
 
 def peer(axis, step):
@@ -62,19 +62,26 @@
     steps_of = [lax.axis_size(axis) - 1 for _, axis, _ in items]
     firsts = [sum(steps_of[:which]) for which in range(count)]
     total = sum(steps_of)
+    spread = [kind in ("gather", "total") for kind, _, _ in items]
+    summed = [kind in ("total", "reduce") for kind, _, _ in items]
+    landed = [
+        (lax.axis_size(axis),) + (array.shape if spread[which] else array.shape[1:])
+        for which, (_, axis, array) in enumerate(items)
+    ]
 
     def body(*refs):
-        ins, outs = refs[:count], refs[count : 2 * count]
-        send_sem, recv_sem, local_sem = refs[2 * count :]
+        ins, outs, rest = refs[:count], refs[count : 2 * count], list(refs[2 * count :])
+        send_sem, recv_sem = rest.pop(0), rest.pop(0)
+        slots = [rest.pop(0) if summed[which] else outs[which] for which in range(count)]
         greet(axes)
         copies = []
-        for which, (kind, axis, _) in enumerate(items):
+        for which, (_, axis, _) in enumerate(items):
             me = lax.axis_index(axis)
             for step in range(1, lax.axis_size(axis)):
                 to = peer(axis, step)
                 copy = pltpu.make_async_remote_copy(
-                    src_ref=ins[which] if kind == "gather" else ins[which].at[to],
-                    dst_ref=outs[which].at[me],
+                    src_ref=ins[which] if spread[which] else ins[which].at[to],
+                    dst_ref=slots[which].at[me],
                     send_sem=send_sem.at[firsts[which] + step - 1],
                     recv_sem=recv_sem.at[firsts[which] + step - 1],
                     device_id={axis: to},
@@ -82,35 +89,36 @@
                 )
                 copy.start()
                 copies.append(copy)
-        for which, (kind, axis, _) in enumerate(items):
+        for which, (_, axis, _) in enumerate(items):
             me = lax.axis_index(axis)
-            copy = pltpu.make_async_copy(
-                ins[which] if kind == "gather" else ins[which].at[me],
-                outs[which].at[me],
-                local_sem.at[which],
-            )
-            copy.start()
-            copies.append(copy)
+            slots[which][me] = ins[which][...] if spread[which] else ins[which][me]
         for copy in copies:
             copy.wait()
+        for which, (_, axis, _) in enumerate(items):
+            if summed[which]:
+                value = slots[which][0].astype(jnp.float32)
+                for index in range(1, lax.axis_size(axis)):
+                    value += slots[which][index].astype(jnp.float32)
+                outs[which][...] = value.astype(outs[which].dtype)
 
     shapes = [
-        jax.ShapeDtypeStruct(
-            (lax.axis_size(axis),) + array.shape if kind == "gather" else array.shape, array.dtype
-        )
-        for kind, axis, array in items
+        jax.ShapeDtypeStruct(landed[which][1:] if summed[which] else landed[which], array.dtype)
+        for which, (_, _, array) in enumerate(items)
     ]
     return pl.pallas_call(
         body,
         out_shape=shapes,
-        in_specs=[ANY] * count,
-        out_specs=[ANY] * count,
-        scratch_shapes=[
-            pltpu.SemaphoreType.DMA((total,)),
-            pltpu.SemaphoreType.DMA((total,)),
-            pltpu.SemaphoreType.DMA((count,)),
+        in_specs=[VMEM] * count,
+        out_specs=[VMEM] * count,
+        scratch_shapes=[pltpu.SemaphoreType.DMA((total,)), pltpu.SemaphoreType.DMA((total,))]
+        + [
+            pltpu.VMEM(landed[which], array.dtype)
+            for which, (_, _, array) in enumerate(items)
+            if summed[which]
         ],
-        compiler_params=pltpu.CompilerParams(collective_id=collective_id, has_side_effects=True),
+        compiler_params=pltpu.CompilerParams(
+            collective_id=collective_id, has_side_effects=True, vmem_limit_bytes=50 << 20
+        ),
         name="exchange",
     )(*[array for _, _, array in items])
 
@@ -119,7 +127,7 @@
     dp_size, ctx_size = lax.axis_size("dp"), lax.axis_size("ctx")
     far, near = dp_size - 1, ctx_size - 1
 
-    def body(x, c, out, c_out, send_a, recv_a, send_b, recv_b, send_c, recv_c, local_sem):
+    def body(x, c, out, c_out, send_a, recv_a, send_b, recv_b, send_c, recv_c):
         row, col = lax.axis_index("dp"), lax.axis_index("ctx")
         greet(("dp", "ctx"))
         first, conds, later = [], [], []
@@ -135,10 +143,8 @@
             )
             copy.start()
             first.append(copy)
-        own = pltpu.make_async_copy(x, out.at[row], local_sem.at[0])
-        own.start()
-        own_cond = pltpu.make_async_copy(c, c_out.at[row], local_sem.at[1])
-        own_cond.start()
+        out[row] = x[...]
+        c_out[row] = c[...]
         for step in range(1, dp_size):
             first[step - 1].wait_recv()
             origin = source("dp", step)
@@ -158,8 +164,6 @@
             copy.wait_send()
         for copy in conds + later:
             copy.wait()
-        own.wait()
-        own_cond.wait()
 
     dma = pltpu.SemaphoreType.DMA
     return pl.pallas_call(
@@ -168,8 +172,8 @@
             jax.ShapeDtypeStruct((dp_size,) + shard.shape, shard.dtype),
             jax.ShapeDtypeStruct((dp_size,) + cond_rows.shape, cond_rows.dtype),
         ],
-        in_specs=[ANY] * 2,
-        out_specs=[ANY] * 2,
+        in_specs=[VMEM] * 2,
+        out_specs=[VMEM] * 2,
         scratch_shapes=[
             dma((far,)),
             dma((far,)),
@@ -177,15 +181,16 @@
             dma((far * near,)),
             dma((far,)),
             dma((far,)),
-            dma((2,)),
         ],
-        compiler_params=pltpu.CompilerParams(collective_id=collective_id, has_side_effects=True),
+        compiler_params=pltpu.CompilerParams(
+            collective_id=collective_id, has_side_effects=True, vmem_limit_bytes=50 << 20
+        ),
         name="gather_weights",
     )(shard, cond_rows)
 
 
 def tensor_total(collective_id, partial_rows):
-    return jnp.sum(exchange(collective_id, ("gather", "tensor", partial_rows))[0], axis=0)
+    return exchange(collective_id, ("total", "tensor", partial_rows))[0]
 
 
 def dot_f32(left, right, left_dim, right_dim):
@@ -227,8 +232,8 @@
     my_start = lax.axis_index("dp") * shard_rows
     silu_part = lax.dynamic_slice(silu_all, (0, my_start), (dp_size * latents, shard_rows))
     mod_part = dot_f32(low(silu_part), ada_w[0], 1, 0)
-    (mod_parts,) = exchange(1, ("scatter", "dp", mod_part.reshape(dp_size, latents, 6 * width)))
-    modulation = jnp.sum(mod_parts, axis=0) + f32(ada_b[0])
+    (mod_sum,) = exchange(1, ("reduce", "dp", mod_part.reshape(dp_size, latents, 6 * width)))
+    modulation = mod_sum + f32(ada_b[0])
     shift_attn, scale_attn, gate_attn, shift_mlp, scale_mlp, gate_mlp = split_six(modulation, width)
     live_mask = f32(jnp.arange(latents) < latent_count[0])[:, None, None]
 
@@ -271,11 +276,11 @@
     pre_grad = low(gelu_pull(dot_f32(mlp_grad, fc2_t, 1, 0))[0])
     both = exchange(
         4,
-        ("gather", "tensor", dot_f32(hidden_act, fc2_t, 1, 1)),
-        ("gather", "tensor", dot_f32(pre_grad, fc1_full, 1, 1)),
-    )
-    branch_mlp = (jnp.sum(both[0], axis=0) + f32(fc2_b[0])).reshape(latents, span, width)
-    mlp_in_grad = jnp.sum(both[1], axis=0).reshape(latents, span, width)
+        ("total", "tensor", dot_f32(hidden_act, fc2_t, 1, 1)),
+        ("total", "tensor", dot_f32(pre_grad, fc1_full, 1, 1)),
+    )
+    branch_mlp = (both[0] + f32(fc2_b[0])).reshape(latents, span, width)
+    mlp_in_grad = both[1].reshape(latents, span, width)
     mixed = low((middle + gate_mlp * branch_mlp) * live_mask)
     gate_mlp_grad = jnp.sum(stream_grad * branch_mlp, axis=1)
     fc2_b_grad = jnp.sum(f32(mlp_grad), axis=0)
@@ -301,8 +306,7 @@
         2, latents, heads, ctx_size, span, head_size
     )
     pair_grad = jnp.transpose(pair_grad, (3, 1, 4, 0, 2, 5)).reshape(ctx_size, rows, 2 * inner)
-    (pair_parts,) = exchange(5, ("scatter", "ctx", pair_grad))
-    pair_own = low(jnp.sum(f32(pair_parts), axis=0))
+    (pair_own,) = exchange(5, ("reduce", "ctx", pair_grad))
     flat_qkv = jnp.concatenate(
         [jnp.transpose(query_grad, (0, 2, 1, 3)).reshape(rows, inner), pair_own], axis=1
     )
@@ -321,19 +325,19 @@
     )[None]
 
     all_grads = low(jnp.concatenate([qkv_grad, out_grad_t, fc1_grad, fc2_grad_t], axis=1))
-    all_grads = jnp.transpose(all_grads.reshape(dp_size, ctx_size, part, columns), (1, 0, 2, 3))
-    grad_parts, mod_parts, bias_parts = exchange(
-        7, ("scatter", "ctx", all_grads), ("gather", "ctx", mod_grad), ("gather", "ctx", biases)
-    )
-    grad_part = low(jnp.sum(f32(grad_parts), axis=0))
-    grad_parts, mod_all, bias_parts = exchange(
+    all_grads = jnp.transpose(all_grads.reshape(dp_size, ctx_size, part, columns), (1, 0, 2, 3)).reshape(
+        ctx_size, dp_size * part, columns
+    )
+    grad_part, mod_sum, bias_sum = exchange(
+        7, ("reduce", "ctx", all_grads), ("total", "ctx", mod_grad), ("total", "ctx", biases)
+    )
+    grad_own, mod_all, bias_total = exchange(
         8,
-        ("scatter", "dp", grad_part),
-        ("gather", "dp", jnp.sum(mod_parts, axis=0)),
-        ("gather", "dp", jnp.sum(bias_parts, axis=0)),
-    )
-    grad_own = low(jnp.sum(f32(grad_parts), axis=0))
-    bias_total = jnp.sum(bias_parts, axis=0)[0]
+        ("reduce", "dp", grad_part.reshape(dp_size, part, columns)),
+        ("gather", "dp", mod_sum),
+        ("total", "dp", bias_sum),
+    )
+    bias_total = bias_total[0]
     mod_all = mod_all.reshape(dp_size * latents, 6 * width)
     ada_b_grad = jnp.sum(mod_all, axis=0)
     ada_w_grad = jnp.dot(silu_part.T, mod_all, precision=PRECISE)

time: 254 us -> 194 us (0.76)
  Pallas kernels: 159 us -> 110 us
  local copies, waits for them, and re-layouts: 29.6 us -> 43 us
  other arithmetic: 34.5 us -> 21.3 us
  matrix products: 27.3 us -> 16.9 us
    pallas_call x9, Pallas kernels: 132 us -> 83.8 us  [exchange(): pl.pallas_call(body, out_shape=shapes, in_specs=[VMEM] * count, out_specs...]
    reduce_sum x11 -> x3, other arithmetic: 13.7 us -> 3.88 us  [the longest x1 1.85 us: per_device(): scale_mlp_grad = jnp.sum(mlp_in_grad * normed_mlp, axis=1)]
    dot_general x13, matrix products: 18.8 us -> 9.59 us  [dot_f32(): lax.dot_general(left, right, (((left_dim,), (right_dim,)), ((), ())), pre...]
    slice x3, local copies, waits for them, and re-layouts: 1.76 us -> 7.24 us  [per_device(): key_rows, value_rows = (pairs[0], pairs[1])]
    squeeze x2, local copies, waits for them, and re-layouts: 0.95 us -> 4.43 us  [per_device(): key_rows, value_rows = (pairs[0], pairs[1])]
    reshape x1, local copies, waits for them, and re-layouts: 0.85 us -> 3.51 us  [per_device(): pairs = pairs.reshape(ctx_size, latents, span, 2, heads, head_size)]
    unnamed x61 -> x94, local copies, waits for them, and re-layouts: 4.11 us -> 5.58 us
where the time goes in v2:
time: 194 us; the launch traced here: 193 us
  Pallas kernels  110 us (57%)
  local copies, waits for them, and re-layouts  43 us (22%)
  other arithmetic  21.3 us (11%)
  matrix products  16.9 us (9%)
  between operations  2.24 us (1%)
    pallas_call x9, Pallas kernels, exchange(): pl.pallas_call(body, out_shape=shapes, in_specs=[VMEM] * count, out_specs...  83.8 us
    pallas_call x1, Pallas kernels, gather_weights(): pl.pallas_call(body, out_shape=[jax.ShapeDtypeStruct((dp_size,) + shard.s...  26 us
    dot_general x13, matrix products, dot_f32(): lax.dot_general(left, right, (((left_dim,), (right_dim,)), ((), ())), pre...  9.59 us
    slice x3, local copies, waits for them, and re-layouts, per_device(): key_rows, value_rows = (pairs[0], pairs[1])  7.24 us
    unnamed x94, local copies, waits for them, and re-layouts  5.58 us
    dot_general x6, matrix products, batched(): return jnp.einsum(equation, left, right, preferred_element_type=jnp.float32)  4.92 us
    squeeze x2, local copies, waits for them, and re-layouts, per_device(): key_rows, value_rows = (pairs[0], pairs[1])  4.43 us

profile of v2, /device:TPU:0, one launch (start us, length us, event | category | flops | bytes accessed | tf_op | source)
XLA Modules:
  0.0 193.3 jit_solution(1771026462353953757)
XLA Ops:
  1.4 1.3 convert_reduce_fusion.8
  2.7 1.3 convert_reduce_fusion.7
  3.9 1.0 convert_reduce_fusion.2
  5.0 1.1 fusion.44
  7.1 1.3 convert_reduce_fusion.6
  9.9 0.9 copy.46
  10.8 1.1 copy.45
  12.1 1.1 concatenate.35.x
  13.2 26.0 %gather_weights.1 = (bf16[4,4,24,2304]{3,2,1,0:T(8,128)(2,1)S(1)}, f32[4,4,384]{2,1,0:T(4,128)S(1)}) custom-call(bf16[4,24,2304]{2,1,0:T(8,128)(2,1)S(1)} %concatenate.35.x, f32[4,384]{1,0:T(4,128)S(1)} %fusion.78.c), custom_call_target="tpu_custom_call" | custom-call | tf_op jit(solution)/shard_map/gather_weights/pallas_call | solution.py:169
  39.5 6.6 %exchange.9 = f32[4,2304]{1,0:T(4,128)S(1)} custom-call(f32[4,4,2304]{2,1,0:T(4,128)S(1)} %fusion.32.refs_0_), custom_call_target="tpu_custom_call" | custom-call | tf_op jit(solution)/shard_map/exchange/pallas_call | solution.py:108
  50.7 10.5 %exchange.10 = bf16[4,256,384]{2,1,0:T(8,128)(2,1)S(1)} custom-call(bf16[256,384]{1,0:T(8,128)(2,1)S(1)} %slice.121.refs_0_), custom_call_target="tpu_custom_call" | custom-call | tf_op jit(solution)/shard_map/exchange/pallas_call | solution.py:108
  61.2 1.2 copy.50
  62.4 3.5 %reshape.220 = bf16[4,4,64,2,3,64]{2,1,5,4,3,0:T(4,128)(2,1)} reshape(bf16[4,256,384]{1,2,0:T(8,128)(2,1)} %copy.50) | data formatting | bytes 1572864 | tf_op jit(solution)/shard_map/reshape | solution.py:248
  65.9 3.0 %fusion.83 = (bf16[1,4,3,4,64,64]{4,1,5,2,0,3:T(4,128)(2,1)S(1)}, bf16[1,4,3,4,64,64]{4,1,5,2,0,3:T(4,128)(2,1)}) fusion(bf16[2,4,3,4,64,64]{4,1,5,2,0,3:T(4,128)(2,1)} %bitcast.191), kind=kLoop, calls=%fused_computation.165 | loop fusion | bytes 1572864 | tf_op jit(solution)/shard_map/slice | solution.py:252
  68.9 1.5 copy.51
  70.4 1.9 squeeze.33
  72.3 2.8 %copy.52 = bf16[1,4,3,4,64,64]{4,3,5,2,1,0:T(4,128)(2,1)} copy(bf16[1,4,3,4,64,64]{4,1,5,2,0,3:T(4,128)(2,1)} %get-tuple-element.81) | data formatting | bytes 786432 | tf_op jit(solution)/shard_map/slice | solution.py:252
  75.1 2.5 %squeeze.34 = bf16[4,3,256,64]{2,3,1,0:T(8,128)(2,1)} reshape(bf16[1,4,3,4,64,64]{4,3,5,2,1,0:T(4,128)(2,1)} %copy.52) | data formatting | bytes 786432 | tf_op jit(solution)/shard_map/squeeze | solution.py:252
  78.8 1.1 fusion.51
  80.8 1.8 exchange.11
  84.3 1.0 convolution_add_fusion
  85.3 1.3 convert_reduce_fusion
  86.6 1.1 convolution_convert_fusion.1
  88.2 1.3 convolution_convert_fusion
  89.9 2.4 %exchange.12 = (f32[256,384]{1,0:T(8,128)S(1)}, f32[256,384]{1,0:T(8,128)S(1)}) custom-call(f32[256,384]{1,0:T(8,128)S(1)} %fusion.17.refs_0_, f32[256,384]{1,0:T(8,128)S(1)} %fusion.21.refs_1_), custom_call_target="tpu_custom_call" | custom-call | tf_op jit(solution)/shard_map/exchange/pallas_call | solution.py:108
  93.0 1.3 div.72
  94.4 1.7 multiply_reduce_fusion
  96.1 1.8 fusion.52
  98.0 2.3 %convert_reduce_fusion.4 = (f32[384]{0:T(512)}, bf16[4,64,384]{2,1,0:T(8,128)(2,1)S(1)}, f32[4,64,384]{2,1,0:T(8,128)}, bf16[4,64,384]{2,1,0:T(8,128)(2,1)}) fusion(f32[4,384]{1,0:T(4,128)S(1)} %get-tuple-element.109, f32[4,64]{1,0:T(4,128)S(1)} %broadcast_multiply_fusion.1, f32[4,64,384]{2,1,0:T(8,128)S(1)} %copy-done.3, ...), kind=kLoop, calls=%fused_computation.84 | loop fusion | flops 1769088 | bytes 2186768 | tf_op jit(solution)/shard_map/reduce_sum | solution.py:295
  100.8 1.1 fusion.45
  101.9 1.8 fusion.1
  103.8 1.1 convolution_convert_fusion.3
  106.0 0.9 convolution_convert_fusion.4
  107.9 1.8 stack.10
  110.3 1.3 maximum_bitcast_fusion
  111.6 1.2 reshape.230
  113.2 12.2 %exchange.13 = bf16[256,384]{1,0:T(8,128)(2,1)S(1)} custom-call(bf16[4,256,384]{2,1,0:T(8,128)(2,1)S(1)} %copy.60.refs_0_), custom_call_target="tpu_custom_call" | custom-call | tf_op jit(solution)/shard_map/exchange/pallas_call | solution.py:108
  125.5 1.5 fusion.34.refs_0_
  127.0 1.8 exchange.14
  129.6 3.6 %concatenate.38 = bf16[4,4,24,2304]{3,2,1,0:T(8,128)(2,1)} concatenate(bf16[4,4,24,576]{3,2,1,0:T(8,128)(2,1)S(1)} %convolution_convert_fusion.2, bf16[4,4,24,192]{3,2,1,0:T(8,128)(2,1)S(1)} %copy-done.16, bf16[4,4,24,768]{3,2,1,0:T(8,128)(2,1)S(1)} %copy-done.10, bf16[4,4,24,768]{3,2,1,0:T(8,128)(2,1)} %convolution_convert_fusion), dimensions={3} | concatenate | bytes 3538944 | tf_op jit(solution)/shard_map/concatenate | solution.py:327
  133.4 1.6 copy.67
  135.4 1.0 multiply_reduce_fusion.1
  136.5 24.9 %exchange.15 = (bf16[96,2304]{1,0:T(8,128)(2,1)S(1)}, f32[4,2304]{1,0:T(4,128)S(1)}, f32[1,1920]{1,0:T(1,128)S(1)}) custom-call(bf16[4,96,2304]{2,1,0:T(8,128)(2,1)S(1)} %bitcast.178, f32[4,2304]{1,0:T(4,128)S(1)} %constant_dynamic-update-slice_fusion.refs_1_, f32[1,1920]{1,0:T(1,128)S(1)} %broadcast_in_dim.13.refs_2_), custom_call_target="tpu_custom_call" | custom-call | tf_op jit(solution)/shard_map/exchange/pallas_call | solution.py:108
  161.4 16.9 %exchange.16 = (bf16[24,2304]{1,0:T(8,128)(2,1)S(1)}, f32[4,4,2304]{2,1,0:T(4,128)S(1)}, f32[1,1920]{1,0:T(1,128)S(1)}) custom-call(bf16[4,24,2304]{2,1,0:T(8,128)(2,1)S(1)} %bitcast.188, f32[4,2304]{1,0:T(4,128)S(1)} %get-tuple-element.30.refs_1_, f32[1,1920]{1,0:T(1,128)S(1)} %get-tuple-element.31.refs_2_), custom_call_target="tpu_custom_call" | custom-call | tf_op jit(solution)/shard_map/exchange/pallas_call | solution.py:108
  181.4 6.6 %exchange.17 = (bf16[4,24,2304]{2,1,0:T(8,128)(2,1)S(1)}, f32[4,4,96]{2,1,0:T(4,128)S(1)}) custom-call(bf16[24,2304]{1,0:T(8,128)(2,1)S(1)} %get-tuple-element.32.refs_0_, f32[4,4,96]{2,1,0:T(4,128)S(1)} %fusion.30.refs_1_), custom_call_target="tpu_custom_call" | custom-call | tf_op jit(solution)/shard_map/exchange/pallas_call | solution.py:108
  188.7 1.9 convolution_bitcast_fusion
  191.5 0.9 slice_bitcast_fusion
  192.4 0.9 copy.94
  (171 shorter events, 22.0 us)
Async XLA Ops:
  0.6 38.6 %copy-start = (bf16[1,96,2304]{2,1,0:T(8,128)(2,1)S(1)}, bf16[1,96,2304]{2,1,0:T(8,128)(2,1)}, u32[]{:S(2)}) copy-start(bf16[1,96,2304]{2,1,0:T(8,128)(2,1)} %param.18) | copy-start | bytes 1327108
  1.4 46.4 %copy-start.39 = (f32[4]{0:T(128)}, f32[4]{0:T(128)S(1)}, u32[]{:S(2)}) copy-start(f32[4]{0:T(128)S(1)} %compare_convert_fusion) | copy-start | bytes 52
  6.1 40.7 %copy-start.27 = (f32[4,64]{1,0:T(4,128)}, f32[4,64]{1,0:T(4,128)S(1)}, u32[]{:S(2)}) copy-start(f32[4,64]{1,0:T(4,128)S(1)} %add_rsqrt_fusion.1) | copy-start | bytes 3076
  8.4 38.4 %copy-start.4 = (bf16[4,64,384]{2,1,0:T(8,128)(2,1)S(1)}, bf16[4,64,384]{2,1,0:T(8,128)(2,1)}, u32[]{:S(2)}) copy-start(bf16[4,64,384]{2,1,0:T(8,128)(2,1)} %param.14) | copy-start | bytes 589828
  12.1 35.7 %copy-start.11 = (bf16[4,64,384]{2,1,0:T(8,128)(2,1)S(1)}, bf16[4,64,384]{2,1,0:T(8,128)(2,1)}, u32[]{:S(2)}) copy-start(bf16[4,64,384]{2,1,0:T(8,128)(2,1)} %param.17) | copy-start | bytes 589828
  39.2 61.1 %copy-start.1 = (bf16[4,4,24,2304]{3,2,1,0:T(8,128)(2,1)}, bf16[4,4,24,2304]{3,2,1,0:T(8,128)(2,1)S(1)}, u32[]{:S(2)}) copy-start(bf16[4,4,24,2304]{3,2,1,0:T(8,128)(2,1)S(1)} %get-tuple-element.26) | copy-start | bytes 5308420
  48.5 1.3 copy-start.17
  70.4 7.2 %copy-start.13 = (bf16[4,64,3,64]{3,2,1,0:T(4,128)(2,1)S(1)}, bf16[4,64,3,64]{3,2,1,0:T(4,128)(2,1)}, u32[]{:S(2)}) copy-start(bf16[4,64,3,64]{3,2,1,0:T(4,128)(2,1)} %reshape.249) | copy-start | bytes 294916
  72.3 5.6 %copy-start.6 = (bf16[4,3,256,64]{2,3,1,0:T(8,128)(2,1)}, bf16[4,3,256,64]{2,3,1,0:T(8,128)(2,1)S(1)}, u32[]{:S(2)}) copy-start(bf16[4,3,256,64]{2,3,1,0:T(8,128)(2,1)S(1)} %squeeze.33) | copy-start | bytes 1179652
  77.6 1.2 copy-start.20
  77.9 0.9 copy-start.8
  77.9 2.0 %copy-start.22 = (f32[4,3,64]{2,1,0:T(4,128)}, f32[4,3,64]{2,1,0:T(4,128)S(1)}, u32[]{:S(2)}) copy-start(f32[4,3,64]{2,1,0:T(4,128)S(1)} %get-tuple-element.98) | copy-start | bytes 9220
  78.3 1.6 copy-start.24
  79.9 2.7 %copy-start.33 = (f32[384]{0:T(512)S(1)}, f32[384]{0:T(512)}, u32[]{:S(2)}) copy-start(f32[384]{0:T(512)} %convert_reduce_fusion.8) | copy-start | bytes 4612
  80.4 3.1 %copy-start.32 = (f32[4,384]{1,0:T(4,128)S(1)}, f32[4,384]{1,0:T(4,128)}, u32[]{:S(2)}) copy-start(f32[4,384]{1,0:T(4,128)} %get-tuple-element.104) | copy-start | bytes 18436
  82.7 2.7 %copy-start.18 = (bf16[4,64,384]{2,1,0:T(8,128)(2,1)S(1)}, bf16[4,64,384]{2,1,0:T(8,128)(2,1)}, u32[]{:S(2)}) copy-start(bf16[4,64,384]{2,1,0:T(8,128)(2,1)} %copy-done.17) | copy-start | bytes 589828
  82.8 0.8 copy-start.2
  83.6 0.6 copy-start.26
  86.6 1.5 copy-start.21
  94.4 3.6 %copy-start.3 = (f32[4,64,384]{2,1,0:T(8,128)S(1)}, f32[4,64,384]{2,1,0:T(8,128)}, u32[]{:S(2)}) copy-start(f32[4,64,384]{2,1,0:T(8,128)} %copy-done.2) | copy-start | bytes 1179652
  94.4 3.6 %copy-start.12 = (bf16[4,64,384]{2,1,0:T(8,128)(2,1)S(1)}, bf16[4,64,384]{2,1,0:T(8,128)(2,1)}, u32[]{:S(2)}) copy-start(bf16[4,64,384]{2,1,0:T(8,128)(2,1)} %param.17) | copy-start | bytes 589828
  94.4 3.6 %copy-start.38 = (f32[4,64]{1,0:T(4,128)S(1)}, f32[4,64]{1,0:T(4,128)}, u32[]{:S(2)}) copy-start(f32[4,64]{1,0:T(4,128)} %div.72) | copy-start | bytes 3076
  97.9 2.9 %copy-start.25 = (f32[4,3,64]{2,1,0:T(4,128)S(1)}, f32[4,3,64]{2,1,0:T(4,128)}, u32[]{:S(2)}) copy-start(f32[4,3,64]{2,1,0:T(4,128)} %copy-done.24) | copy-start | bytes 9220
  98.0 3.9 %copy-start.23 = (f32[4,3,64]{2,1,0:T(4,128)S(1)}, f32[4,3,64]{2,1,0:T(4,128)}, u32[]{:S(2)}) copy-start(f32[4,3,64]{2,1,0:T(4,128)} %copy-done.22) | copy-start | bytes 9220
  101.9 1.9 copy-start.9
  103.8 1.1 copy-start.7
  103.8 1.4 copy-start.14
  113.2 15.9 %copy-start.19 = (bf16[384,256]{1,0:T(8,128)(2,1)S(1)}, bf16[384,256]{1,0:T(8,128)(2,1)}, u32[]{:S(2)}) copy-start(bf16[384,256]{1,0:T(8,128)(2,1)} %copy.62) | copy-start | bytes 589828
  125.5 4.1 %copy-start.10 = (bf16[4,4,24,768]{3,2,1,0:T(8,128)(2,1)S(1)}, bf16[4,4,24,768]{3,2,1,0:T(8,128)(2,1)}, u32[]{:S(2)}) copy-start(bf16[4,4,24,768]{3,2,1,0:T(8,128)(2,1)} %convolution_convert_fusion.1) | copy-start | bytes 1769476
  125.5 4.1 %copy-start.16 = (bf16[4,4,24,192]{3,2,1,0:T(8,128)(2,1)S(1)}, bf16[4,4,24,192]{3,2,1,0:T(8,128)(2,1)}, u32[]{:S(2)}) copy-start(bf16[4,4,24,192]{3,2,1,0:T(8,128)(2,1)} %convolution_convert_fusion.4) | copy-start | bytes 442372
  129.6 3.7 %copy-start.36 = (f32[384]{0:T(512)S(1)}, f32[384]{0:T(512)}, u32[]{:S(2)}) copy-start(f32[384]{0:T(512)} %get-tuple-element.71) | copy-start | bytes 4612
  129.6 3.7 %copy-start.37 = (f32[384]{0:T(512)S(1)}, f32[384]{0:T(512)}, u32[]{:S(2)}) copy-start(f32[384]{0:T(512)} %get-tuple-element.73) | copy-start | bytes 4612
  129.6 3.7 %copy-start.40 = (f32[768]{0:T(1024)S(1)}, f32[768]{0:T(1024)}, u32[]{:S(2)}) copy-start(f32[768]{0:T(1024)} %get-tuple-element.102) | copy-start | bytes 9220
  133.4 1.7 copy-start.5
  133.4 1.7 copy-start.28
  133.4 2.0 %copy-start.15 = (f32[4,64,384]{2,1,0:T(8,128)S(1)}, f32[4,64,384]{2,1,0:T(8,128)}, u32[]{:S(2)}) copy-start(f32[4,64,384]{2,1,0:T(8,128)} %get-tuple-element.75) | copy-start | bytes 1179652
  133.4 2.0 %copy-start.34 = (f32[384]{0:T(512)S(1)}, f32[384]{0:T(512)}, u32[]{:S(2)}) copy-start(f32[384]{0:T(512)} %convert_reduce_fusion.8) | copy-start | bytes 4612
  135.1 1.4 copy-start.31
  135.1 1.4 copy-start.30
  135.1 1.4 copy-start.29
  136.5 51.6 %copy-start.35 = (bf16[4,384]{1,0:T(4,128)(2,1)S(1)}, bf16[4,384]{1,0:T(4,128)(2,1)}, u32[]{:S(2)}) copy-start(bf16[4,384]{1,0:T(4,128)(2,1)} %param.15) | copy-start | bytes 9220

commit v3 on v2

--- a/solution.py
+++ b/solution.py
@@ -199,6 +199,89 @@
     )
 
 
+def attention_weights(queries, keys):
+    scores = dot_f32(queries, keys, 1, 1) * float(HD) ** (-0.5)
+    weights = jnp.exp(scores - jnp.max(scores, axis=-1, keepdims=True))
+    return weights, jnp.sum(weights, axis=-1, keepdims=True)
+
+
+def attention_blocks(latents, span, inner):
+    for latent in range(latents):
+        for start in range(0, inner, HD):
+            yield slice(latent * span, (latent + 1) * span), start
+
+
+def attention_forward(qkv_rows, pairs, latents):
+    rows, inner = qkv_rows.shape[0], qkv_rows.shape[1] // 3
+    span = rows // latents
+    keys_total = pairs.shape[0] * span
+
+    def body(q_ref, kv_ref, o_ref, low_ref):
+        for here, start in attention_blocks(latents, span, inner):
+            queries = q_ref[here, start : start + HD]
+            keys = kv_ref[:, here, start : start + HD].reshape(keys_total, HD)
+            values = kv_ref[:, here, inner + start : inner + start + HD].reshape(keys_total, HD)
+            weights, row_sum = attention_weights(queries, keys)
+            out = dot_f32(weights.astype(jnp.bfloat16), values, 1, 0) / row_sum
+            o_ref[here, start : start + HD] = out
+            low_ref[here, start : start + HD] = out.astype(jnp.bfloat16)
+
+    return pl.pallas_call(
+        body,
+        out_shape=[
+            jax.ShapeDtypeStruct((rows, inner), jnp.float32),
+            jax.ShapeDtypeStruct((rows, inner), jnp.bfloat16),
+        ],
+        in_specs=[VMEM] * 2,
+        out_specs=[VMEM] * 2,
+        compiler_params=pltpu.CompilerParams(vmem_limit_bytes=50 << 20),
+        name="attention_forward",
+    )(qkv_rows, pairs)
+
+
+def attention_backward(qkv_rows, pairs, attended, attn_grad, latents):
+    rows, inner = attended.shape
+    span = rows // latents
+    ctx_size = pairs.shape[0]
+    keys_total = ctx_size * span
+    scale = float(HD) ** (-0.5)
+
+    def body(q_ref, kv_ref, o_ref, g_ref, q_grad_ref, pair_ref):
+        for here, start in attention_blocks(latents, span, inner):
+            queries = q_ref[here, start : start + HD]
+            keys = kv_ref[:, here, start : start + HD].reshape(keys_total, HD)
+            values = kv_ref[:, here, inner + start : inner + start + HD].reshape(keys_total, HD)
+            upstream = g_ref[here, start : start + HD]
+            wide = upstream.astype(jnp.float32)
+            weights, row_sum = attention_weights(queries, keys)
+            delta = jnp.sum(wide * o_ref[here, start : start + HD], axis=-1, keepdims=True)
+            prob_grad = dot_f32(upstream, values, 1, 1)
+            score_grad = (weights / row_sum * (prob_grad - delta)).astype(jnp.bfloat16)
+            q_grad_ref[here, start : start + HD] = (
+                scale * dot_f32(score_grad, keys, 1, 0)
+            ).astype(jnp.bfloat16)
+            key_grad = (scale * dot_f32(score_grad, queries, 0, 0)).astype(jnp.bfloat16)
+            value_grad = dot_f32(
+                weights.astype(jnp.bfloat16), (wide / row_sum).astype(jnp.bfloat16), 0, 0
+            ).astype(jnp.bfloat16)
+            pair_ref[:, here, start : start + HD] = key_grad.reshape(ctx_size, span, HD)
+            pair_ref[:, here, inner + start : inner + start + HD] = value_grad.reshape(
+                ctx_size, span, HD
+            )
+
+    return pl.pallas_call(
+        body,
+        out_shape=[
+            jax.ShapeDtypeStruct((rows, inner), jnp.bfloat16),
+            jax.ShapeDtypeStruct(pairs.shape, jnp.bfloat16),
+        ],
+        in_specs=[VMEM] * 4,
+        out_specs=[VMEM] * 2,
+        compiler_params=pltpu.CompilerParams(vmem_limit_bytes=50 << 20),
+        name="attention_backward",
+    )(qkv_rows, pairs, attended, attn_grad)
+
+
 def per_device(
     tokens, cond, latent_count, cotangent, ada_w, ada_b, qkv_w, qv_b,
     out_w, out_b, fc1_w, fc1_b, fc2_w, fc2_b,
@@ -243,25 +326,8 @@
     bias_pair = f32(qv_b[0]).reshape(2, inner)
     bias_row = jnp.concatenate([bias_pair[0], jnp.zeros_like(bias_pair[0]), bias_pair[1]])
     qkv_rows = low(dot_f32(attn_in, qkv_full, 1, 0) + bias_row)
-    queries = qkv_rows[:, :inner].reshape(latents, span, heads, head_size)
     (pairs,) = exchange(2, ("gather", "ctx", qkv_rows[:, inner:]))
-    pairs = pairs.reshape(ctx_size, latents, span, 2, heads, head_size)
-    pairs = jnp.transpose(pairs, (3, 1, 4, 0, 2, 5)).reshape(
-        2, latents, heads, ctx_size * span, head_size
-    )
-    key_rows, value_rows = pairs[0], pairs[1]
-    queries = jnp.transpose(queries, (0, 2, 1, 3))
-    scale = float(HD) ** (-0.5)
-
-    def batched(equation, left, right):
-        return jnp.einsum(equation, left, right, preferred_element_type=jnp.float32)
-
-    scores = batched("lhqe,lhke->lhqk", queries, key_rows) * scale
-    weights = jnp.exp(scores - jnp.max(scores, axis=-1, keepdims=True))
-    row_sum = jnp.sum(weights, axis=-1, keepdims=True)
-    weights_low = low(weights)
-    attended = batched("lhqk,lhke->lhqe", weights_low, value_rows) / row_sum
-    attended_low = jnp.transpose(low(attended), (0, 2, 1, 3)).reshape(rows, inner)
+    attended, attended_low = attention_forward(qkv_rows, pairs, latents)
     branch_attn = (
         tensor_total(3, dot_f32(attended_low, out_t, 1, 1)) + f32(out_b[0])
     ).reshape(latents, span, width)
@@ -294,22 +360,10 @@
     branch_grad = low(middle_grad * gate_attn).reshape(rows, width)
     out_b_grad = jnp.sum(f32(branch_grad), axis=0)
     out_grad_t = dot_f32(branch_grad, attended_low, 0, 0)
-    attn_grad = low(dot_f32(branch_grad, out_t, 1, 0)).reshape(latents, span, heads, head_size)
-    attn_grad = jnp.transpose(attn_grad, (0, 2, 1, 3))
-    delta = jnp.sum(f32(attn_grad) * attended, axis=-1, keepdims=True)
-    prob_grad = batched("lhqe,lhke->lhqk", attn_grad, value_rows)
-    score_grad = low(weights / row_sum * (prob_grad - delta))
-    query_grad = low(scale * batched("lhqk,lhke->lhqe", score_grad, key_rows))
-    key_grad = scale * batched("lhqk,lhqe->lhke", score_grad, queries)
-    value_grad = batched("lhqk,lhqe->lhke", weights_low, low(f32(attn_grad) / row_sum))
-    pair_grad = low(jnp.stack([key_grad, value_grad])).reshape(
-        2, latents, heads, ctx_size, span, head_size
-    )
-    pair_grad = jnp.transpose(pair_grad, (3, 1, 4, 0, 2, 5)).reshape(ctx_size, rows, 2 * inner)
+    attn_grad = low(dot_f32(branch_grad, out_t, 1, 0))
+    query_grad, pair_grad = attention_backward(qkv_rows, pairs, attended, attn_grad, latents)
     (pair_own,) = exchange(5, ("reduce", "ctx", pair_grad))
-    flat_qkv = jnp.concatenate(
-        [jnp.transpose(query_grad, (0, 2, 1, 3)).reshape(rows, inner), pair_own], axis=1
-    )
+    flat_qkv = jnp.concatenate([query_grad, pair_own], axis=1)
     qkv_sums = jnp.sum(f32(flat_qkv), axis=0)
     qkv_grad = dot_f32(attn_in, flat_qkv, 0, 0)
     attn_in_grad = tensor_total(6, dot_f32(flat_qkv, qkv_full, 1, 1)).reshape(latents, span, width)

time: 194 us -> 169 us (0.87)
  local copies, waits for them, and re-layouts: 43 us -> 15.6 us
  Pallas kernels: 110 us -> 118 us
  other arithmetic: 21.3 us -> 16 us
    pallas_call x0 -> x2, Pallas kernels: none -> 8 us  [the longest x1 4.98 us: attention_backward(): pl.pallas_call(body, out_shape=[jax.ShapeDtypeStruct((rows, inner), jnp.b...]
    slice x4 -> x0, local copies, waits for them, and re-layouts: 7.25 us -> none  [the longest x3 7.24 us: per_device(): key_rows, value_rows = (pairs[0], pairs[1])]
    reshape x9 -> x0, local copies, waits for them, and re-layouts: 6.75 us -> none  [the longest x1 3.51 us: per_device(): pairs = pairs.reshape(ctx_size, latents, span, 2, heads, head_size)]
    dot_general x6 -> x0, matrix products: 4.92 us -> none  [batched(): return jnp.einsum(equation, left, right, preferred_element_type=jnp.float32)]
    squeeze x2 -> x0, local copies, waits for them, and re-layouts: 4.43 us -> none  [per_device(): key_rows, value_rows = (pairs[0], pairs[1])]
    dot_general x13, matrix products: 9.59 us -> 13.3 us  [dot_f32(): lax.dot_general(left, right, (((left_dim,), (right_dim,)), ((), ())), pre...]
    another operation x4 -> x0, local copies, waits for them, and re-layouts: 3.37 us -> none  [per_device(): jnp.stack([key_grad, value_grad])]
    unnamed x94 -> x66, local copies, waits for them, and re-layouts: 5.58 us -> 4.05 us
where the time goes in v3:
time: 169 us; the launch traced here: 168 us
  Pallas kernels  118 us (70%)
  matrix products  16.4 us (10%)
  other arithmetic  16 us (9%)
  local copies, waits for them, and re-layouts  15.6 us (9%)
  between operations  2.09 us (1%)
    pallas_call x9, Pallas kernels, exchange(): pl.pallas_call(body, out_shape=shapes, in_specs=[VMEM] * count, out_specs...  83.8 us
    pallas_call x1, Pallas kernels, gather_weights(): pl.pallas_call(body, out_shape=[jax.ShapeDtypeStruct((dp_size,) + shard.s...  26 us
    dot_general x13, matrix products, dot_f32(): lax.dot_general(left, right, (((left_dim,), (right_dim,)), ((), ())), pre...  13.3 us
    pallas_call x1, Pallas kernels, attention_backward(): pl.pallas_call(body, out_shape=[jax.ShapeDtypeStruct((rows, inner), jnp.b...  4.98 us
    unnamed x66, local copies, waits for them, and re-layouts  4.05 us

profile of v3, /device:TPU:0, one launch (start us, length us, event | category | flops | bytes accessed | tf_op | source)
XLA Modules:
  0.0 167.9 jit_solution(2911747573919198413)
XLA Ops:
  1.4 0.7 convert_reduce_fusion.8
  2.1 1.3 convert_reduce_fusion.7
  3.4 1.0 convert_reduce_fusion.2
  4.4 1.1 fusion.37
  5.6 0.7 convert_element_type.93
  6.5 0.7 convert_reduce_fusion.6
  7.2 0.7 fusion.55.c
  8.0 0.7 convert_reduce_fusion.5
  8.7 0.9 copy.55
  9.6 1.1 copy.54
  11.0 1.1 concatenate.33.x
  12.1 26.0 %gather_weights.1 = (bf16[4,4,24,2304]{3,2,1,0:T(8,128)(2,1)S(1)}, f32[4,4,384]{2,1,0:T(4,128)S(1)}) custom-call(bf16[4,24,2304]{2,1,0:T(8,128)(2,1)S(1)} %concatenate.33.x, f32[4,384]{1,0:T(4,128)S(1)} %fusion.55.c), custom_call_target="tpu_custom_call" | custom-call | tf_op jit(solution)/shard_map/gather_weights/pallas_call | solution.py:169
  38.9 6.6 %exchange.9 = f32[4,2304]{1,0:T(4,128)S(1)} custom-call(f32[4,4,2304]{2,1,0:T(4,128)S(1)} %fusion.25.refs_0_), custom_call_target="tpu_custom_call" | custom-call | tf_op jit(solution)/shard_map/exchange/pallas_call | solution.py:108
  45.9 0.8 copy.58
  46.7 0.7 convert_reduce_fusion.3
  47.4 0.8 copy.63
  48.7 10.5 %exchange.10.kv_ref = bf16[4,256,384]{2,1,0:T(8,128)(2,1)S(1)} custom-call(bf16[256,384]{1,0:T(8,128)(2,1)S(1)} %slice.106.refs_0_), custom_call_target="tpu_custom_call" | custom-call | tf_op jit(solution)/shard_map/exchange/pallas_call | solution.py:108
  59.3 3.0 %attention_forward.1 = (f32[256,192]{1,0:T(8,128)S(1)}, bf16[256,192]{1,0:T(8,128)(2,1)S(1)}) custom-call(bf16[256,576]{1,0:T(8,128)(2,1)S(1)} %fusion.q_ref, bf16[4,256,384]{2,1,0:T(8,128)(2,1)S(1)} %exchange.10.kv_ref), custom_call_target="tpu_custom_call" | custom-call | tf_op jit(solution)/shard_map/attention_forward/pallas_call | solution.py:229
  62.3 1.3 fusion.45.refs_0_
  63.6 1.8 %exchange.11 = f32[256,384]{1,0:T(8,128)S(1)} custom-call(f32[256,384]{1,0:T(8,128)S(1)} %fusion.45.refs_0_), custom_call_target="tpu_custom_call" | custom-call | tf_op jit(solution)/shard_map/exchange/pallas_call | solution.py:108
  66.2 1.4 convolution_add_fusion
  67.6 2.5 %convert_reduce_fusion = (f32[768]{0:T(1024)}, bf16[256,768]{1,0:T(8,128)(2,1)S(1)}) fusion(f32[256,768]{1,0:T(8,128)S(1)} %convolution_add_fusion, bf16[256,384]{1,0:T(8,128)(2,1)S(1)} %bitcast.141, bf16[384,2304]{1,0:T(8,128)(2,1)} %bitcast.126), kind=kOutput, calls=%fused_computation.18 | convolution fusion | flops 155319552 | bytes 1969152 | tf_op jit(solution)/shard_map/dot_general | solution.py:197
  70.1 1.1 convolution_convert_fusion.1
  71.7 1.3 convolution_convert_fusion
  73.4 2.4 %exchange.12 = (f32[256,384]{1,0:T(8,128)S(1)}, f32[256,384]{1,0:T(8,128)S(1)}) custom-call(f32[256,384]{1,0:T(8,128)S(1)} %fusion.10.refs_0_, f32[256,384]{1,0:T(8,128)S(1)} %fusion.14.refs_1_), custom_call_target="tpu_custom_call" | custom-call | tf_op jit(solution)/shard_map/exchange/pallas_call | solution.py:108
  76.5 1.3 div.40
  77.8 1.7 %multiply_reduce_fusion = (f32[4,384]{1,0:T(4,128)}, f32[256,384]{1,0:T(8,128)S(1)}) fusion(bf16[4,64,384]{2,1,0:T(8,128)(2,1)} %param.17, f32[4]{0:T(128)} %copy-done.25, f32[256,384]{1,0:T(8,128)S(1)} %get-tuple-element.32, f32[384]{0:T(512)} %convert_reduce_fusion.7), kind=kLoop, calls=%fused_computation.65 | loop fusion | flops 489984 | bytes 990736 | tf_op jit(solution)/shard_map/reduce_sum | solution.py:351
  79.6 0.9 fusion.42
  80.6 1.8 %convert_reduce_fusion.4 = (f32[384]{0:T(512)S(1)}, bf16[4,64,384]{2,1,0:T(8,128)(2,1)S(1)}, f32[4,64,384]{2,1,0:T(8,128)}, bf16[4,64,384]{2,1,0:T(8,128)(2,1)}) fusion(f32[4,384]{1,0:T(4,128)S(1)} %get-tuple-element.124, f32[4,64]{1,0:T(4,128)S(1)} %broadcast_multiply_fusion.1, f32[4,64,384]{2,1,0:T(8,128)S(1)} %get-tuple-element.100, ...), kind=kLoop, calls=%fused_computation.64 | loop fusion | flops 1769088 | bytes 2186768 | tf_op jit(solution)/shard_map/reduce_sum | solution.py:361
  82.3 1.3 convolution_convert_fusion.4
  83.8 5.0 %attention_backward.1 = (bf16[256,192]{1,0:T(8,128)(2,1)S(1)}, bf16[4,256,384]{2,1,0:T(8,128)(2,1)S(1)}) custom-call(bf16[256,576]{1,0:T(8,128)(2,1)S(1)} %fusion.q_ref, bf16[4,256,384]{2,1,0:T(8,128)(2,1)S(1)} %exchange.10.kv_ref, f32[256,192]{1,0:T(8,128)S(1)} %get-tuple-element.34.o_ref, bf16[256,192]{1,0:T(8,128)(2,1)S(1)} %copy.57.g_ref), custom_call_target="tpu_custom_call" | custom-call | tf_op jit(solution)/shard_map/attention_backward/pallas_call | solution.py:272
  88.8 12.2 %exchange.13 = bf16[256,384]{1,0:T(8,128)(2,1)S(1)} custom-call(bf16[4,256,384]{2,1,0:T(8,128)(2,1)S(1)} %get-tuple-element.36.refs_0_), custom_call_target="tpu_custom_call" | custom-call | tf_op jit(solution)/shard_map/exchange/pallas_call | solution.py:108
  101.1 1.5 fusion.27.refs_0_
  102.6 1.8 %exchange.14 = f32[256,384]{1,0:T(8,128)S(1)} custom-call(f32[256,384]{1,0:T(8,128)S(1)} %fusion.27.refs_0_), custom_call_target="tpu_custom_call" | custom-call | tf_op jit(solution)/shard_map/exchange/pallas_call | solution.py:108
  104.7 1.3 convolution_convert_fusion.2
  106.5 1.0 multiply_reduce_fusion.1
  108.0 2.3 %concatenate.36 = bf16[4,4,24,2304]{3,2,1,0:T(8,128)(2,1)S(1)} concatenate(bf16[4,4,24,576]{3,2,1,0:T(8,128)(2,1)} %convolution_convert_fusion.2, bf16[4,4,24,192]{3,2,1,0:T(8,128)(2,1)S(1)} %convolution_convert_fusion.3, bf16[4,4,24,768]{3,2,1,0:T(8,128)(2,1)S(1)} %copy-done.6, bf16[4,4,24,768]{3,2,1,0:T(8,128)(2,1)} %convolution_convert_fusion), dimensions={3} | concatenate | bytes 3538944 | tf_op jit(solution)/shard_map/concatenate | solution.py:381
  110.5 24.9 %exchange.15 = (bf16[96,2304]{1,0:T(8,128)(2,1)S(1)}, f32[4,2304]{1,0:T(4,128)S(1)}, f32[1,1920]{1,0:T(1,128)S(1)}) custom-call(bf16[4,96,2304]{2,1,0:T(8,128)(2,1)S(1)} %bitcast.121, f32[4,2304]{1,0:T(4,128)S(1)} %constant_dynamic-update-slice_fusion.refs_1_, f32[1,1920]{1,0:T(1,128)S(1)} %broadcast_in_dim.13.refs_2_), custom_call_target="tpu_custom_call" | custom-call | tf_op jit(solution)/shard_map/exchange/pallas_call | solution.py:108
  135.4 16.9 %exchange.16 = (bf16[24,2304]{1,0:T(8,128)(2,1)S(1)}, f32[4,4,2304]{2,1,0:T(4,128)S(1)}, f32[1,1920]{1,0:T(1,128)S(1)}) custom-call(bf16[4,24,2304]{2,1,0:T(8,128)(2,1)S(1)} %bitcast.131, f32[4,2304]{1,0:T(4,128)S(1)} %get-tuple-element.38.refs_1_, f32[1,1920]{1,0:T(1,128)S(1)} %get-tuple-element.39.refs_2_), custom_call_target="tpu_custom_call" | custom-call | tf_op jit(solution)/shard_map/exchange/pallas_call | solution.py:108
  152.3 0.6 slice.97
  153.5 0.6 copy.68
  154.7 0.6 broadcast_in_dim.15
  155.3 6.6 %exchange.17 = (bf16[4,24,2304]{2,1,0:T(8,128)(2,1)S(1)}, f32[4,4,96]{2,1,0:T(4,128)S(1)}) custom-call(bf16[24,2304]{1,0:T(8,128)(2,1)S(1)} %get-tuple-element.40.refs_0_, f32[4,4,96]{2,1,0:T(4,128)S(1)} %fusion.23.refs_1_), custom_call_target="tpu_custom_call" | custom-call | tf_op jit(solution)/shard_map/exchange/pallas_call | solution.py:108
  162.0 0.6 fusion.54
  162.6 2.6 %convolution_bitcast_fusion = f32[1,96,2304]{2,1,0:T(8,128)} fusion(f32[16,2304]{1,0:T(8,128)S(1)} %reshape.196, f32[16,384]{1,0:T(8,128)} %copy-done.12, s32[]{:T(128)S(6)} %select_n.3), kind=kOutput, calls=%fused_computation | convolution fusion | flops 42467328 | bytes 1040388 | tf_op jit(solution)/shard_map/dot_general | solution.py:397
  165.4 0.7 copy.83
  166.2 0.9 slice_bitcast_fusion
  167.0 0.9 copy.82
  (116 shorter events, 7.2 us)
Async XLA Ops:
  0.6 38.1 %copy-start = (bf16[1,96,2304]{2,1,0:T(8,128)(2,1)S(1)}, bf16[1,96,2304]{2,1,0:T(8,128)(2,1)}, u32[]{:S(2)}) copy-start(bf16[1,96,2304]{2,1,0:T(8,128)(2,1)} %param.18) | copy-start | bytes 1327108
  1.4 45.3 %copy-start.25 = (f32[4]{0:T(128)}, f32[4]{0:T(128)S(1)}, u32[]{:S(2)}) copy-start(f32[4]{0:T(128)S(1)} %compare_convert_fusion) | copy-start | bytes 52
  2.1 63.4 %copy-start.20 = (f32[384]{0:T(512)}, f32[384]{0:T(512)S(1)}, u32[]{:S(2)}) copy-start(f32[384]{0:T(512)S(1)} %convert_reduce_fusion.8) | copy-start | bytes 4612
  4.4 41.3 %copy-start.14 = (f32[4,64]{1,0:T(4,128)}, f32[4,64]{1,0:T(4,128)S(1)}, u32[]{:S(2)}) copy-start(f32[4,64]{1,0:T(4,128)S(1)} %broadcast_multiply_fusion.3) | copy-start | bytes 3076
  5.6 40.1 %copy-start.17 = (f32[4,64]{1,0:T(4,128)}, f32[4,64]{1,0:T(4,128)S(1)}, u32[]{:S(2)}) copy-start(f32[4,64]{1,0:T(4,128)S(1)} %add_rsqrt_fusion.1) | copy-start | bytes 3076
  7.2 38.5 %copy-start.3 = (bf16[4,64,384]{2,1,0:T(8,128)(2,1)S(1)}, bf16[4,64,384]{2,1,0:T(8,128)(2,1)}, u32[]{:S(2)}) copy-start(bf16[4,64,384]{2,1,0:T(8,128)(2,1)} %param.14) | copy-start | bytes 589828
  10.9 35.8 %copy-start.7 = (bf16[4,64,384]{2,1,0:T(8,128)(2,1)S(1)}, bf16[4,64,384]{2,1,0:T(8,128)(2,1)}, u32[]{:S(2)}) copy-start(bf16[4,64,384]{2,1,0:T(8,128)(2,1)} %param.17) | copy-start | bytes 589828
  38.0 10.6 %copy-start.1 = (bf16[4,4,24,2304]{3,2,1,0:T(8,128)(2,1)}, bf16[4,4,24,2304]{3,2,1,0:T(8,128)(2,1)S(1)}, u32[]{:S(2)}) copy-start(bf16[4,4,24,2304]{3,2,1,0:T(8,128)(2,1)S(1)} %get-tuple-element.30) | copy-start | bytes 5308420
  38.1 0.7 copy-start.12
  59.3 6.2 %copy-start.4 = (bf16[4,64,384]{2,1,0:T(8,128)(2,1)S(1)}, bf16[4,64,384]{2,1,0:T(8,128)(2,1)}, u32[]{:S(2)}) copy-start(bf16[4,64,384]{2,1,0:T(8,128)(2,1)} %param.14) | copy-start | bytes 589828
  65.6 4.5 %copy-start.13 = (f32[4,64]{1,0:T(4,128)}, f32[4,64]{1,0:T(4,128)S(1)}, u32[]{:S(2)}) copy-start(f32[4,64]{1,0:T(4,128)S(1)} %broadcast_multiply_fusion.2) | copy-start | bytes 3076
  65.9 4.3 %copy-start.16 = (f32[4,64]{1,0:T(4,128)}, f32[4,64]{1,0:T(4,128)S(1)}, u32[]{:S(2)}) copy-start(f32[4,64]{1,0:T(4,128)S(1)} %add_rsqrt_fusion) | copy-start | bytes 3076
  67.6 3.7 %copy-start.2 = (bf16[4,4,24,2304]{3,2,1,0:T(8,128)(2,1)S(1)}, bf16[4,4,24,2304]{3,2,1,0:T(8,128)(2,1)}, u32[]{:S(2)}) copy-start(bf16[4,4,24,2304]{3,2,1,0:T(8,128)(2,1)} %copy-done.1) | copy-start | bytes 5308420
  70.1 1.5 copy-start.11
  77.8 2.7 %copy-start.8 = (bf16[4,64,384]{2,1,0:T(8,128)(2,1)S(1)}, bf16[4,64,384]{2,1,0:T(8,128)(2,1)}, u32[]{:S(2)}) copy-start(bf16[4,64,384]{2,1,0:T(8,128)(2,1)} %param.17) | copy-start | bytes 589828
  77.8 2.7 %copy-start.24 = (f32[4,64]{1,0:T(4,128)S(1)}, f32[4,64]{1,0:T(4,128)}, u32[]{:S(2)}) copy-start(f32[4,64]{1,0:T(4,128)} %div.40) | copy-start | bytes 3076
  88.7 16.0 %copy-start.10 = (bf16[384,256]{1,0:T(8,128)(2,1)S(1)}, bf16[384,256]{1,0:T(8,128)(2,1)}, u32[]{:S(2)}) copy-start(bf16[384,256]{1,0:T(8,128)(2,1)} %copy.58) | copy-start | bytes 589828
  101.0 5.1 %copy-start.23 = (f32[384]{0:T(512)S(1)}, f32[384]{0:T(512)}, u32[]{:S(2)}) copy-start(f32[384]{0:T(512)} %get-tuple-element.92) | copy-start | bytes 4612
  101.0 5.1 %copy-start.26 = (f32[768]{0:T(1024)S(1)}, f32[768]{0:T(1024)}, u32[]{:S(2)}) copy-start(f32[768]{0:T(1024)} %get-tuple-element.117) | copy-start | bytes 9220
  101.0 5.2 %copy-start.5 = (bf16[4,64,384]{2,1,0:T(8,128)(2,1)S(1)}, bf16[4,64,384]{2,1,0:T(8,128)(2,1)}, u32[]{:S(2)}) copy-start(bf16[4,64,384]{2,1,0:T(8,128)(2,1)} %param.14) | copy-start | bytes 589828
  101.0 5.2 %copy-start.15 = (f32[4,64]{1,0:T(4,128)S(1)}, f32[4,64]{1,0:T(4,128)}, u32[]{:S(2)}) copy-start(f32[4,64]{1,0:T(4,128)} %copy-done.14) | copy-start | bytes 3076
  101.0 5.2 %copy-start.18 = (f32[4,64]{1,0:T(4,128)S(1)}, f32[4,64]{1,0:T(4,128)}, u32[]{:S(2)}) copy-start(f32[4,64]{1,0:T(4,128)} %copy-done.17) | copy-start | bytes 3076
  102.5 4.0 %copy-start.9 = (f32[4,64,384]{2,1,0:T(8,128)S(1)}, f32[4,64,384]{2,1,0:T(8,128)}, u32[]{:S(2)}) copy-start(f32[4,64,384]{2,1,0:T(8,128)} %get-tuple-element.96) | copy-start | bytes 1179652
  102.5 4.0 %copy-start.21 = (f32[384]{0:T(512)S(1)}, f32[384]{0:T(512)}, u32[]{:S(2)}) copy-start(f32[384]{0:T(512)} %copy-done.20) | copy-start | bytes 4612
  104.7 2.9 %copy-start.19 = (f32[4,384]{1,0:T(4,128)S(1)}, f32[4,384]{1,0:T(4,128)}, u32[]{:S(2)}) copy-start(f32[4,384]{1,0:T(4,128)} %get-tuple-element.97) | copy-start | bytes 18436
  106.2 1.8 %copy-start.6 = (bf16[4,4,24,768]{3,2,1,0:T(8,128)(2,1)S(1)}, bf16[4,4,24,768]{3,2,1,0:T(8,128)(2,1)}, u32[]{:S(2)}) copy-start(bf16[4,4,24,768]{3,2,1,0:T(8,128)(2,1)} %convolution_convert_fusion.1) | copy-start | bytes 1769476
  110.5 51.6 %copy-start.22 = (bf16[4,384]{1,0:T(4,128)(2,1)S(1)}, bf16[4,384]{1,0:T(4,128)(2,1)}, u32[]{:S(2)}) copy-start(bf16[4,384]{1,0:T(4,128)(2,1)} %param.15) | copy-start | bytes 9220
